TPU v7x, 1024 devices: a whole 4x4x32 slice. The times are simulated.
1024 devices in a mesh: dp: 32 (over z_lo, x), expert: 32 (over z_hi, y, core).
Axes of the slice: x: 4, y: 4, z: 32 (z_hi: 4, z_lo: 8; z = z_hi * 8 + z_lo), core: 2. Of those that a mesh axis runs over, the one named last changes fastest.
Arguments:
- out_grad: bfloat16 [131072, 4096], P(('dp', 'expert')), may hold values from -6 to 6
- expert_ids: int32 [131072, 1], P(('dp', 'expert')), may hold values from 0 to 31; in each aligned block of 128 rows (0 to 127, 128 to 255, ...) at most 6 rows name the same one
- gate_values: bfloat16 [131072, 1], P(('dp', 'expert')), may hold values from 0.19921875 to 1
- down_weight: bfloat16 [32, 4096, 768], P('expert'), may hold values from -0.21875 to 0.21875
- gate_up: bfloat16 [32, 32, 192, 1536], P('dp', 'expert'), may hold values from -6 to 6
Outputs:
- weight_grad: bfloat16 [32, 4096, 768], P('expert', 'dp')
- gate_up_grad: bfloat16 [32, 32, 192, 1536], P('dp', 'expert')
- gate_grad: float32 [131072, 1], P(('dp', 'expert'))
Inputs may be any that keep to these rules, and one draw needn't show every extreme that they name: `expert_ids`: within the 128 tokens of one device (aligned blocks of rows), no expert is named more than 6 times; some block names some expert exactly 6 times.
All inputs are finite; a program needn't handle non-finite values.
Results may differ from a plain program's by a relative error of at most 0.0057.
Values may be sent and summed in bfloat16 or wider, within the bound.
No kernel may reach another device: no remote copies, remote signals or barrier semaphores. Data moves between devices by JAX's collectives and lax.ppermute only.
A program may use at most 64 MiB of HBM per device.

v0:
```python
import jax
import jax.numpy as jnp
from jax import lax
from jax.sharding import PartitionSpec as P


def per_device(out_grad, expert_ids, gate_values, down_weight, gate_up):
    experts = lax.axis_size("expert")
    saved_acts = gate_up[0, 0]
    slot_count = saved_acts.shape[0]
    capacity = slot_count // experts
    hidden_units = saved_acts.shape[1] // 2
    route_count = expert_ids.shape[1]
    pair_count = expert_ids.shape[0] * route_count
    chosen = expert_ids.reshape(pair_count)
    onehot = (chosen[:, None] == jnp.arange(experts, dtype=jnp.int32)[None, :]).astype(jnp.int32)
    before = jnp.cumsum(onehot, axis=0) - onehot
    places = chosen * capacity + jnp.sum(before * onehot, axis=1)
    token_of = jnp.arange(pair_count, dtype=jnp.int32) // route_count
    send_rows = (
        jnp.zeros((experts * capacity, out_grad.shape[1]), jnp.bfloat16)
        .at[places]
        .set(out_grad[token_of])
    )
    send_gates = (
        jnp.zeros((experts * capacity,), jnp.bfloat16)
        .at[places]
        .set(gate_values.reshape(pair_count))
    )
    received, route_gate = (
        lax.all_to_all(send_rows, "expert", split_axis=0, concat_axis=0, tiled=True),
        lax.all_to_all(send_gates, "expert", split_axis=0, concat_axis=0, tiled=True),
    )
    gates_wide = route_gate.astype(jnp.float32)[:, None]
    scaled = (gates_wide * received.astype(jnp.float32)).astype(jnp.bfloat16)
    gate_act = saved_acts[:, :hidden_units].astype(jnp.float32)
    up_act = saved_acts[:, hidden_units:].astype(jnp.float32)
    sigmoid_val = jax.nn.sigmoid(gate_act)
    silu_val = gate_act * sigmoid_val
    hidden = (silu_val * up_act).astype(jnp.bfloat16)
    weight = down_weight[0]
    share_rows = lax.psum_scatter(
        lax.dot_general(
            scaled, hidden, (((0,), (0,)), ((), ())), preferred_element_type=jnp.float32
        ),
        "dp",
        scatter_dimension=0,
        tiled=True,
    )
    weight_share = share_rows.astype(jnp.bfloat16)
    raw_grad = jnp.dot(received, weight, preferred_element_type=jnp.float32)
    hidden_grad = gates_wide * raw_grad
    outputs = lax.dot_general(
        hidden, weight, (((1,), (1,)), ((), ())), preferred_element_type=jnp.float32
    )
    score = jnp.sum(received.astype(jnp.float32) * outputs, axis=1)
    gate_part = hidden_grad * up_act * sigmoid_val * (1.0 + gate_act * (1.0 - sigmoid_val))
    up_part = hidden_grad * silu_val
    gu_grad = jnp.concatenate([gate_part, up_part], axis=1).astype(jnp.bfloat16)
    returned = lax.all_to_all(score, "expert", split_axis=0, concat_axis=0, tiled=True)
    route_grad = returned[places].reshape(expert_ids.shape)
    return (weight_share[None], gu_grad[None, None], route_grad)


def solution(mesh):
    return jax.shard_map(
        per_device,
        mesh=mesh,
        in_specs=(
            P(("dp", "expert"), None),
            P(("dp", "expert"), None),
            P(("dp", "expert"), None),
            P("expert", None, None),
            P("dp", "expert", None, None),
        ),
        out_specs=(
            P("expert", "dp", None),
            P("dp", "expert", None, None),
            P(("dp", "expert"), None),
        ),
        check_vma=False,
    )
```

profile of v0, /device:TPU:24, one launch (start us, length us, event | category | flops | bytes accessed | tf_op | source)
XLA Modules:
  0.0 554.8 jit_solution(4294764931133611386)
XLA Ops:
  7.2 0.0 copy-start
  7.2 0.8 fusion.30
  8.0 0.2 reduce_window_sum.11
  8.2 0.8 select_reduce_fusion
  9.0 0.7 fusion.31
  9.7 1.5 scatter_custom_fusion
  11.2 0.7 all_to_all.30
  11.9 31.4 %all-to-all-start = ((bf16[32,6,1]{1,2,0:T(2,128)(2,1)}), bf16[32,6,1]{1,2,0:T(2,128)(2,1)S(1)}, u32[]{:S(2)}, u32[]{:S(2)}) async-start(bf16[32,6,1]{1,2,0:T(2,128)(2,1)} %all_to_all.30), calls=%async_computation | async-start | bytes 32768 | tf_op jit(solution)/shard_map/all_to_all | solution.py:32
  43.3 0.0 copy-done
  43.3 5.6 %scatter_custom_fusion.1 = bf16[192,4096]{1,0:T(8,128)(2,1)S(1)} fusion(s32[128]{0:T(128)S(1)} %fusion.31, bf16[128,4096]{1,0:T(8,128)(2,1)S(1)} %copy-done, s32[1024]{0:T(1024)S(1)} %pad_clamp_fusion.1, bf16[]{:T(256)} %constant.13.clone.1), kind=kCustom, calls=%fused_computation.15 | custom fusion | bytes 1572866 | tf_op jit(solution)/shard_map/scatter | solution.py:23
  48.9 1.6 all_to_all.24
  50.5 15.1 %all-to-all-done = bf16[32,6,1]{1,2,0:T(2,128)(2,1)S(1)} async-done(((bf16[32,6,1]{1,2,0:T(2,128)(2,1)}), bf16[32,6,1]{1,2,0:T(2,128)(2,1)S(1)}, u32[]{:S(2)}, u32[]{:S(2)}) %all-to-all-start) | async-done | bytes 416 | tf_op jit(solution)/shard_map/all_to_all | solution.py:32
  65.5 9.1 %all-to-all-start.1 = ((bf16[32,6,4096]{2,1,0:T(8,128)(2,1)}), bf16[32,6,4096]{2,1,0:T(8,128)(2,1)S(1)}, u32[]{:S(2)}, u32[]{:S(2)}) async-start(bf16[32,6,4096]{2,1,0:T(8,128)(2,1)} %all_to_all.24), calls=%async_computation.1 | async-start | bytes 4194304 | tf_op jit(solution)/shard_map/all_to_all | solution.py:31
  74.7 0.0 reduce-scatter.2.cloned.1.call-start
  74.7 0.1 convert_reduce_fusion
  74.8 0.1 reshape.61
  74.9 188.6 %all-to-all-done.1 = bf16[32,6,4096]{2,1,0:T(8,128)(2,1)S(1)} async-done(((bf16[32,6,4096]{2,1,0:T(8,128)(2,1)}), bf16[32,6,4096]{2,1,0:T(8,128)(2,1)S(1)}, u32[]{:S(2)}, u32[]{:S(2)}) %all-to-all-start.1) | async-done | bytes 1572896 | tf_op jit(solution)/shard_map/all_to_all | solution.py:31
  263.5 1.5 all_to_all.26
  265.0 8.1 %fusion.8 = f32[4096,768]{1,0:T(8,128)} fusion(bf16[192,4096]{1,0:T(8,128)(2,1)} %all_to_all.26, f32[192]{0:T(256)S(1)} %reshape.61, bf16[192,1536]{1,0:T(8,128)(2,1)} %bitcast.32), kind=kOutput, calls=%fused_computation.11 | convolution fusion | flops 1211498496 | bytes 14746368 | tf_op jit(solution)/shard_map/dot_general | solution.py:43
  273.0 0.0 copy-start.1
  273.0 0.0 copy-start.2
  273.0 0.0 reduce-scatter.2.cloned.1.call-update
  273.1 1.4 copy-done.1
  274.4 0.1 copy-done.2
  274.6 5.1 fusion.11
  279.7 0.7 all_to_all.27
  280.4 17.1 %all-to-all-start.2 = ((f32[32,6,1]{1,2,0:T(1,128)}), f32[32,6,1]{1,2,0:T(1,128)S(1)}, u32[]{:S(2)}, u32[]{:S(2)}) async-start(f32[32,6,1]{1,2,0:T(1,128)} %bitcast.9), calls=%async_computation.3 | async-start | bytes 32768 | tf_op jit(solution)/shard_map/all_to_all | solution.py:60
  297.5 4.3 fusion.29
  301.8 0.9 pad_maximum_fusion
  302.7 17.2 %all-to-all-done.2 = f32[32,6,1]{1,2,0:T(1,128)S(1)} async-done(((f32[32,6,1]{1,2,0:T(1,128)}), f32[32,6,1]{1,2,0:T(1,128)S(1)}, u32[]{:S(2)}, u32[]{:S(2)}) %all-to-all-start.2) | async-done | bytes 800 | tf_op jit(solution)/shard_map/all_to_all | solution.py:60
  319.9 0.5 broadcast.61
  320.4 0.7 reduce.7
  321.1 0.1 all_to_all.29
  321.2 1.8 gather_fusion
  323.0 223.2 %reduce-scatter.2.cloned.1.call-done = f32[128,768]{1,0:T(8,128)} async-done(((f32[4096,768]{1,0:T(8,128)}), f32[128,768]{1,0:T(8,128)}) %reduce-scatter.2.cloned.1.call-update) | async-done | bytes 393232 | tf_op jit(solution)/shard_map/reduce_scatter | solution.py:42
  546.2 1.7 convert_bitcast_fusion
  (3 shorter events, 0.0 us)
Async XLA Ops:
  7.2 36.1 %copy-start = (bf16[128,4096]{1,0:T(8,128)(2,1)S(1)}, bf16[128,4096]{1,0:T(8,128)(2,1)}, u32[]{:S(2)}) copy-start(bf16[128,4096]{1,0:T(8,128)(2,1)} %param.5) | copy-start | bytes 3145732
  11.9 53.6 %all-to-all-start = ((bf16[32,6,1]{1,2,0:T(2,128)(2,1)}), bf16[32,6,1]{1,2,0:T(2,128)(2,1)S(1)}, u32[]{:S(2)}, u32[]{:S(2)}) async-start(bf16[32,6,1]{1,2,0:T(2,128)(2,1)} %all_to_all.30), calls=%async_computation | async-start | bytes 32768 | tf_op jit(solution)/shard_map/all_to_all | solution.py:32
  65.5 198.0 %all-to-all-start.1 = ((bf16[32,6,4096]{2,1,0:T(8,128)(2,1)}), bf16[32,6,4096]{2,1,0:T(8,128)(2,1)S(1)}, u32[]{:S(2)}, u32[]{:S(2)}) async-start(bf16[32,6,4096]{2,1,0:T(8,128)(2,1)} %all_to_all.24), calls=%async_computation.1 | async-start | bytes 4194304 | tf_op jit(solution)/shard_map/all_to_all | solution.py:31
  74.7 471.5 %reduce-scatter.2.cloned.1.call-start = ((), (), s32[]{:S(2)}) async-start(), calls=%async_computation.4 | async-start | bytes 12976128 | tf_op jit(solution)/shard_map/reduce_scatter | solution.py:42
  273.0 1.4 copy-start.1
  273.0 1.5 copy-start.2
  280.4 39.5 %all-to-all-start.2 = ((f32[32,6,1]{1,2,0:T(1,128)}), f32[32,6,1]{1,2,0:T(1,128)S(1)}, u32[]{:S(2)}, u32[]{:S(2)}) async-start(f32[32,6,1]{1,2,0:T(1,128)} %bitcast.9), calls=%async_computation.3 | async-start | bytes 32768 | tf_op jit(solution)/shard_map/all_to_all | solution.py:60
Sparse Core Ops, SparseCore 0:
  273.2 273.0 reduce-scatter.1
where the time goes:
time: 555 us
  waiting for transfers between devices  444 us (80%)
  starting transfers between devices  57.7 us (10%)
  matrix products  17.5 us (3%)
  local copies, waits for them, and re-layouts  15.6 us (3%)
  between operations  14.2 us (3%)
  other arithmetic  5.79 us (1%)
    reduce_scatter x1, waiting for transfers between devices, per_device(): lax.psum_scatter(lax.dot_general(scaled, hidden, (((0,), (0,)), ((), ()))...  223 us
    all_to_all x1, waiting for transfers between devices, per_device(): lax.all_to_all(send_rows, 'expert', split_axis=0, concat_axis=0, tiled=True)  189 us
    all_to_all x1, starting transfers between devices, per_device(): lax.all_to_all(send_gates, 'expert', split_axis=0, concat_axis=0, tiled=T...  31.4 us
    all_to_all x1, waiting for transfers between devices, per_device(): lax.all_to_all(score, 'expert', split_axis=0, concat_axis=0, tiled=True)  17.2 us
    all_to_all x1, starting transfers between devices, per_device(): lax.all_to_all(score, 'expert', split_axis=0, concat_axis=0, tiled=True)  17.1 us
    all_to_all x1, waiting for transfers between devices, per_device(): lax.all_to_all(send_gates, 'expert', split_axis=0, concat_axis=0, tiled=T...  15.1 us
  transfers between devices with their start and end apart: 4, of which 4 were waited for; matrix products, arithmetic and copies ran while one was open for 3% of the time, Pallas kernels for 0%

commit v1 on v0

v1 whole, which is shorter than its diff:
```python
import jax
import jax.numpy as jnp
from jax import lax
from jax.experimental import pallas as pl
from jax.experimental.pallas import tpu as pltpu
from jax.sharding import Mesh
from jax.sharding import PartitionSpec as P

BF16, F32, I32 = jnp.bfloat16, jnp.float32, jnp.int32
ZL, X, ZH, Y, C = 8, 4, 4, 4, 2
E = ZH * Y * C
CAP = 6
TOK = 128
D = 4096
LANES = 128
EXPERT = ("zh", "y", "c")
BLOCK = ZL * CAP
FAN = X * E
ROWS = FAN * CAP
SUB = 16
VMEM = 48 * 1024 * 1024


def pack_kernel(ids_ref, gate_ref, grad_ref, rows_ref, gates_ref, keys, grads):
    ids = ids_ref[...]
    onehot = (lax.broadcasted_iota(I32, (E, TOK), 0) == ids).astype(F32)
    earlier = lax.broadcasted_iota(I32, (TOK, TOK), 0) < lax.broadcasted_iota(I32, (TOK, TOK), 1)
    before = jnp.dot(onehot.astype(BF16), earlier.astype(BF16), preferred_element_type=F32)
    place = jnp.sum(before * onehot, axis=0, keepdims=True).astype(I32)
    line = lax.broadcasted_iota(I32, (E * 8, TOK), 0)
    hit = (line // 8 == ids) & (line % 8 == place)
    picked = jnp.where(hit, gate_ref[...].astype(F32), 0.0).astype(BF16)
    gates_ref[...] = jnp.dot(picked, jnp.ones((TOK, LANES), BF16), preferred_element_type=F32).astype(BF16)
    base = ids * BLOCK + place
    for z in range(ZL):
        keys[:, z * TOK : (z + 1) * TOK] = base + z * CAP
        grads[z * TOK : (z + 1) * TOK, :] = grad_ref[:, z * (X * LANES) : (z + 1) * (X * LANES)]
    step = 8 * BLOCK

    def body(i, carry):
        row = lax.broadcasted_iota(I32, (step, ZL * TOK), 0) + i * step
        take = jnp.where(row == keys[...], 1.0, 0.0).astype(BF16)
        out = jnp.dot(take, grads[...], preferred_element_type=F32).astype(BF16)
        for q in range(X):
            rows_ref[q, pl.ds(pl.multiple_of(i * step, step), step), :] = out[:, q * LANES : (q + 1) * LANES]
        return carry

    lax.fori_loop(0, E * BLOCK // step, body, 0)


def pack(ids, gates, grad):
    return pl.pallas_call(
        pack_kernel,
        out_shape=(
            jax.ShapeDtypeStruct((X, E * BLOCK, LANES), BF16),
            jax.ShapeDtypeStruct((E * 8, LANES), BF16),
        ),
        scratch_shapes=[pltpu.VMEM((1, ZL * TOK), I32), pltpu.VMEM((ZL * TOK, X * LANES), BF16)],
        compiler_params=pltpu.CompilerParams(vmem_limit_bytes=VMEM),
        cost_estimate=pl.CostEstimate(flops=2 * E * BLOCK * ZL * TOK * X * LANES, bytes_accessed=3 << 20, transcendentals=0),
        name="pack",
    )(ids, gates, grad)


def weight_kernel(recv_ref, acts_ref, part_ref, plain_ref, scaled):
    chunks = FAN // SUB
    size = SUB * BLOCK
    group = SUB * CAP
    out = lax.broadcasted_iota(I32, (size, size), 0)
    col = lax.broadcasted_iota(I32, (size, size), 1)
    inner = out % group
    source = (inner // CAP) * BLOCK + (out // group) * CAP + inner % CAP
    order = jnp.where(source == col, 1.0, 0.0).astype(BF16)
    for k in range(chunks):
        sorted_rows = jnp.dot(order, recv_ref[k], preferred_element_type=F32)
        gate = acts_ref[k * group : (k + 1) * group, 768:].astype(F32)
        for z in range(ZL):
            tile = sorted_rows[z * group : (z + 1) * group, :]
            plain_ref[k * group : (k + 1) * group, z * LANES : (z + 1) * LANES] = tile.astype(BF16)
            scaled[k * group : (k + 1) * group, z * LANES : (z + 1) * LANES] = (tile * gate).astype(BF16)
    part_ref[...] = lax.dot_general(
        scaled[...], acts_ref[:, :768], (((0,), (0,)), ((), ())), preferred_element_type=F32
    ).astype(part_ref.dtype)


def weight_part(recv, acts):
    return pl.pallas_call(
        weight_kernel,
        out_shape=(
            jax.ShapeDtypeStruct((ZL * LANES, 768), F32),
            jax.ShapeDtypeStruct((ROWS, ZL * LANES), BF16),
        ),
        scratch_shapes=[pltpu.VMEM((ROWS, ZL * LANES), BF16)],
        compiler_params=pltpu.CompilerParams(vmem_limit_bytes=VMEM),
        cost_estimate=pl.CostEstimate(flops=4 * ROWS * ROWS * ZL * LANES, bytes_accessed=8 << 20, transcendentals=0),
        name="weight_part",
    )(recv, acts)


def cycle(parts, own, n):
    turned = [parts[(n - k) % n] for k in range(n)]
    return lax.dynamic_slice_in_dim(jnp.stack(turned + turned), (n - own) % n, n, 0)


def spread(blocks, axis, n, dim):
    own = lax.axis_index(axis)
    parts = [lax.dynamic_index_in_dim(blocks, own, dim, keepdims=False)]
    for d in range(1, n):
        block = lax.dynamic_index_in_dim(blocks, (own + d) % n, dim, keepdims=False)
        parts.append(lax.ppermute(block, axis, [(i, (i + d) % n) for i in range(n)]))
    return cycle(parts, own, n)


def per_device(out_grad, expert_ids, gate_values, down_weight, gate_up):
    own_x = lax.axis_index("x")
    rows, gates = pack(expert_ids.reshape(1, TOK), gate_values.reshape(1, TOK), out_grad)
    recv = lax.all_to_all(
        rows.reshape(FAN, BLOCK, LANES), ("x",) + EXPERT, split_axis=0, concat_axis=0, tiled=True
    )
    g = spread(gates.reshape(ZH, Y, C, 8, LANES), "c", C, 2)
    g = spread(g, "y", Y, 2)
    g = spread(g, "zh", ZH, 2)
    gate_slots = g[..., :CAP, :].reshape(E * CAP, LANES)

    saved = gate_up[0, 0]
    gate_act = saved[:, :768].astype(F32)
    up_act = saved[:, 768:].astype(F32)
    sigmoid_val = jax.nn.sigmoid(gate_act)
    silu_val = gate_act * sigmoid_val
    hidden = (silu_val * up_act).astype(BF16)
    acts = lax.all_gather(jnp.concatenate([hidden, gate_slots], axis=1), "x", axis=0, tiled=True)

    part, plain = weight_part(recv.reshape(FAN // SUB, SUB * BLOCK, LANES), acts)
    share = lax.psum_scatter(part, "zl", scatter_dimension=0, tiled=True)
    weight_share = share.astype(BF16)

    weight = lax.dynamic_index_in_dim(down_weight.reshape(ZL, X, LANES, 768), own_x, 1, keepdims=False)
    raw_part = jnp.dot(plain, weight.reshape(ZL * LANES, 768), preferred_element_type=F32).astype(BF16)
    raw_parts = lax.all_to_all(
        raw_part.reshape(X, E * CAP, 768), "x", split_axis=0, concat_axis=0, tiled=True
    )
    raw_grad = jnp.sum(raw_parts.astype(F32), axis=0)
    hidden_grad = gate_slots[:, :1].astype(F32) * raw_grad
    gate_part = hidden_grad * up_act * sigmoid_val * (1.0 + gate_act * (1.0 - sigmoid_val))
    up_part = hidden_grad * silu_val
    gu_grad = jnp.concatenate([gate_part, up_part], axis=1).astype(BF16)
    score = jnp.sum(hidden.astype(F32) * raw_grad, axis=1)
    returned = lax.all_to_all(score.reshape(E, CAP), EXPERT, split_axis=0, concat_axis=0, tiled=True)

    chosen = expert_ids.reshape(TOK)
    onehot = (chosen[:, None] == jnp.arange(E, dtype=I32)[None, :]).astype(F32)
    later = jnp.arange(TOK)[:, None] > jnp.arange(TOK)[None, :]
    before = jnp.dot(later.astype(BF16), onehot.astype(BF16), preferred_element_type=F32)
    position = jnp.sum(before * onehot, axis=1).astype(I32)
    slots = chosen * CAP + position
    hit = slots[:, None] == jnp.arange(E * CAP, dtype=I32)[None, :]
    route_grad = jnp.sum(jnp.where(hit, returned.reshape(1, E * CAP), 0.0), axis=1)
    return (weight_share[None], gu_grad[None, None], route_grad.reshape(TOK, 1))


def solution(mesh):
    fine = Mesh(mesh.devices.reshape(ZL, X, ZH, Y, C), ("zl", "x", "zh", "y", "c"))
    dp = ("zl", "x")
    return jax.shard_map(
        per_device,
        mesh=fine,
        in_specs=(
            P(dp + EXPERT, None),
            P(dp + EXPERT, None),
            P(dp + EXPERT, None),
            P(EXPERT, None, None),
            P(dp, EXPERT, None, None),
        ),
        out_specs=(
            P(EXPERT, dp, None),
            P(dp, EXPERT, None, None),
            P(dp + EXPERT, None),
        ),
        check_vma=False,
    )
```

time: 555 us -> 351 us (0.63)
  waiting for transfers between devices: 444 us -> 198 us
  starting transfers between devices: 57.7 us -> 113 us
  matrix products: 17.5 us -> 2.58 us
  Pallas kernels: 0 us -> 10 us
  local copies, waits for them, and re-layouts: 15.6 us -> 6.99 us
    reduce_scatter x1, waiting for transfers between devices: 223 us -> 22 us  [per_device(): share = lax.psum_scatter(part, 'zl', scatter_dimension=0, tiled=True)]
    all_to_all x3, waiting for transfers between devices: 221 us -> 37.4 us  [the longest x1 21.7 us: per_device(): lax.all_to_all(score.reshape(E, CAP), EXPERT, split_axis=0, concat_axis=0...]
    ppermute x0 -> x7, waiting for transfers between devices: none -> 98.5 us  [spread(): lax.ppermute(block, axis, [(i, (i + d) % n) for i in range(n)])]
    ppermute x0 -> x7, starting transfers between devices: none -> 48 us  [spread(): lax.ppermute(block, axis, [(i, (i + d) % n) for i in range(n)])]
    all_gather x0 -> x1, waiting for transfers between devices: none -> 39.8 us  [per_device(): lax.all_gather(jnp.concatenate([hidden, gate_slots], axis=1), 'x', axis=0...]
    dot_general x3 -> x2, matrix products: 17.5 us -> 2.58 us  [the longest x1 2.42 us: per_device(): jnp.dot(plain, weight.reshape(ZL * LANES, 768), preferred_element_type=F32)]
    pallas_call x0 -> x2, Pallas kernels: none -> 10 us  [the longest x1 6.27 us: weight_part(): pl.pallas_call(weight_kernel, out_shape=(jax.ShapeDtypeStruct((ZL * LANES...]
    scatter x2 -> x0, local copies, waits for them, and re-layouts: 7.03 us -> none  [the longest x1 5.56 us: per_device(): send_rows = jnp.zeros((experts * capacity, out_grad.shape[1]), jnp.bfloat...]
  transfers between devices with their start and end apart: 4 -> 12, of which waited for: 4 -> 7; matrix products, arithmetic and copies ran while one was open for 3% -> 3% of each run, Pallas kernels for 0% -> 0%
where the time goes in v1:
time: 351 us; the launch traced here: 350 us
  waiting for transfers between devices  198 us (56%)
  starting transfers between devices  113 us (32%)
  between operations  14.5 us (4%)
  Pallas kernels  10 us (3%)
  local copies, waits for them, and re-layouts  6.99 us (2%)
  other arithmetic  5.59 us (2%)
    ppermute x7, waiting for transfers between devices, spread(): lax.ppermute(block, axis, [(i, (i + d) % n) for i in range(n)])  98.5 us
    ppermute x7, starting transfers between devices, spread(): lax.ppermute(block, axis, [(i, (i + d) % n) for i in range(n)])  48 us
    all_gather x1, waiting for transfers between devices, per_device(): lax.all_gather(jnp.concatenate([hidden, gate_slots], axis=1), 'x', axis=0...  39.8 us
    all_to_all x1, starting transfers between devices, per_device(): lax.all_to_all(rows.reshape(FAN, BLOCK, LANES), ('x',) + EXPERT, split_ax...  35.1 us
    all_to_all x1, starting transfers between devices, per_device(): lax.all_to_all(score.reshape(E, CAP), EXPERT, split_axis=0, concat_axis=0...  25.6 us
    reduce_scatter x1, waiting for transfers between devices, per_device(): share = lax.psum_scatter(part, 'zl', scatter_dimension=0, tiled=True)  22 us
    all_to_all x1, waiting for transfers between devices, per_device(): lax.all_to_all(score.reshape(E, CAP), EXPERT, split_axis=0, concat_axis=0...  21.7 us
    all_to_all x1, waiting for transfers between devices, per_device(): lax.all_to_all(raw_part.reshape(X, E * CAP, 768), 'x', split_axis=0, conc...  15.7 us
  transfers between devices with their start and end apart: 12, of which 7 were waited for; matrix products, arithmetic and copies ran while one was open for 3% of the time, Pallas kernels for 0%

profile of v1, /device:TPU:24, one launch (start us, length us, event | category | flops | bytes accessed | tf_op | source)
XLA Modules:
  0.0 349.9 jit_solution(2331624448057632960)
XLA Ops:
  7.2 0.0 copy-start.1
  7.2 1.2 copy-done.1
  8.4 0.7 copy-done.2
  9.0 0.7 copy-done.3
  9.7 3.8 %pack.1 = (bf16[4,1536,128]{2,1,0:T(8,128)(2,1)}, bf16[256,128]{1,0:T(8,128)(2,1)S(1)}) custom-call(s32[1,128]{1,0:T(1,128)S(1)} %bitcast.73, bf16[1,128]{1,0:T(2,128)(2,1)S(1)} %bitcast.72, bf16[128,4096]{1,0:T(8,128)(2,1)S(1)} %copy-done.1), custom_call_target="tpu_custom_call" | custom-call | flops 1610612736 | bytes 3145728 | tf_op jit(solution)/shard_map/pack/pallas_call | solution.py:52
  13.5 35.1 %all-to-all-start = ((bf16[128,48,128]{2,1,0:T(8,128)(2,1)}), bf16[128,48,128]{2,1,0:T(8,128)(2,1)S(1)}, u32[]{:S(2)}, u32[]{:S(2)}) async-start(bf16[128,48,128]{2,1,0:T(8,128)(2,1)} %bitcast.2), calls=%async_computation | async-start | bytes 3145728 | tf_op jit(solution)/shard_map/all_to_all | solution.py:117
  48.6 0.0 all-gather.2.cloned.1.call-start
  48.7 2.1 collective-permute-start
  50.8 0.2 fusion.1
  51.1 0.7 collective-permute-done
  51.9 2.8 collective-permute-start.1
  54.6 3.4 collective-permute-start.2
  58.1 3.6 %collective-permute-start.3 = (bf16[2,4,8,128]{3,2,0,1:T(8,128)(2,1)S(1)}, bf16[2,4,8,128]{3,2,0,1:T(8,128)(2,1)S(1)}, u32[]{:S(2)}, u32[]{:S(2)}) collective-permute-start(bf16[2,4,8,128]{3,2,0,1:T(8,128)(2,1)S(1)} %bitcast.83), channel_id=1, source_target_pairs={{0,2},{2,4},{4,6},{6,0},{1,3},{3,5},{5,7},{7,1},{8,10},{10,12},{12... | collective-permute-start | bytes 49160 | tf_op jit(solution)/shard_map/ppermute | solution.py:110
  61.7 0.0 collective-permute-done.1
  61.8 0.0 collective-permute-done.2
  61.8 1.9 collective-permute-done.3
  63.8 11.9 %collective-permute-start.4 = (bf16[4,2,8,128]{3,2,1,0:T(8,128)(2,1)S(1)}, bf16[4,2,8,128]{3,2,1,0:T(8,128)(2,1)S(1)}, u32[]{:S(2)}, u32[]{:S(2)}) collective-permute-start(bf16[4,2,8,128]{3,2,1,0:T(8,128)(2,1)S(1)} %get-tuple-element.16), channel_id=1, source_target_pairs={{0,24},{8,0},{16,8},{24,16},{1,25},{9,1},{17,9},{25,17},{2,26},{10... | collective-permute-start | bytes 49160 | tf_op jit(solution)/shard_map/ppermute | solution.py:110
  75.7 12.1 %collective-permute-start.5 = (bf16[4,2,8,128]{3,2,1,0:T(8,128)(2,1)S(1)}, bf16[4,2,8,128]{3,2,1,0:T(8,128)(2,1)S(1)}, u32[]{:S(2)}, u32[]{:S(2)}) collective-permute-start(bf16[4,2,8,128]{3,2,1,0:T(8,128)(2,1)S(1)} %get-tuple-element.15), channel_id=1, source_target_pairs={{0,16},{8,24},{16,0},{24,8},{1,17},{9,25},{17,1},{25,9},{2,18},{10... | collective-permute-start | bytes 49160 | tf_op jit(solution)/shard_map/ppermute | solution.py:110
  87.8 12.1 %collective-permute-start.6 = (bf16[4,2,8,128]{3,2,1,0:T(8,128)(2,1)S(1)}, bf16[4,2,8,128]{3,2,1,0:T(8,128)(2,1)S(1)}, u32[]{:S(2)}, u32[]{:S(2)}) collective-permute-start(bf16[4,2,8,128]{3,2,1,0:T(8,128)(2,1)S(1)} %get-tuple-element.14), channel_id=1, source_target_pairs={{0,8},{8,16},{16,24},{24,0},{1,9},{9,17},{17,25},{25,1},{2,10},{10... | collective-permute-start | bytes 49160 | tf_op jit(solution)/shard_map/ppermute | solution.py:110
  100.0 95.8 %collective-permute-done.4 = bf16[4,2,8,128]{3,2,1,0:T(8,128)(2,1)S(1)} collective-permute-done((bf16[4,2,8,128]{3,2,1,0:T(8,128)(2,1)S(1)}, bf16[4,2,8,128]{3,2,1,0:T(8,128)(2,1)S(1)}, u32[]{:S(2)}, u32[]{:S(2)}) %collective-permute-start.4) | collective-permute-done | bytes 16416 | tf_op jit(solution)/shard_map/ppermute | solution.py:110
  195.8 0.0 collective-permute-done.5
  195.8 0.0 collective-permute-done.6
  196.0 0.8 pad_maximum_fusion.1
  196.7 0.0 all-gather.2.cloned.1.call-update
  196.7 0.0 reduce-scatter.2.cloned.1.call-start
  196.8 39.8 %all-gather.2.cloned.1.call-done.acts_ref = bf16[768,896]{1,0:T(8,128)(2,1)} async-done(((bf16[192,896]{1,0:T(8,128)(2,1)}), bf16[768,896]{1,0:T(8,128)(2,1)}) %all-gather.2.cloned.1.call-update) | async-done | bytes 1376272 | tf_op jit(solution)/shard_map/all_gather | solution.py:131
  236.5 0.0 all-to-all-done
  236.5 1.3 copy-done
  237.9 6.3 %weight_part.1 = (f32[1024,768]{1,0:T(8,128)}, bf16[768,1024]{1,0:T(8,128)(2,1)S(1)}) custom-call(bf16[8,768,128]{2,1,0:T(8,128)(2,1)S(1)} %bitcast.70, bf16[768,896]{1,0:T(8,128)(2,1)S(1)} %copy-done), custom_call_target="tpu_custom_call" | custom-call | flops 2415919104 | bytes 8388608 | tf_op jit(solution)/shard_map/weight_part/pallas_call | solution.py:87
  244.2 0.0 reduce-scatter.2.cloned.1.call-update
  244.2 1.5 constant_dynamic-slice_fusion
  245.7 2.4 convolution_convert_fusion
  248.1 3.7 %all-to-all-start.1 = ((bf16[4,192,768]{2,1,0:T(8,128)(2,1)}), bf16[4,192,768]{2,1,0:T(8,128)(2,1)S(1)}, u32[]{:S(2)}, u32[]{:S(2)}) async-start(bf16[4,192,768]{2,1,0:T(8,128)(2,1)} %bitcast.78), calls=%async_computation.2 | async-start | bytes 2359296 | tf_op jit(solution)/shard_map/all_to_all | solution.py:139
  251.8 0.2 fusion
  252.0 0.1 convert_reduce_fusion.1
  252.1 15.7 %all-to-all-done.1 = bf16[4,192,768]{2,1,0:T(8,128)(2,1)S(1)} async-done(((bf16[4,192,768]{2,1,0:T(8,128)(2,1)}), bf16[4,192,768]{2,1,0:T(8,128)(2,1)S(1)}, u32[]{:S(2)}, u32[]{:S(2)}) %all-to-all-start.1) | async-done | bytes 1179680 | tf_op jit(solution)/shard_map/all_to_all | solution.py:139
  267.8 0.2 convert_reduce_fusion
  268.0 0.5 fusion.10
  268.5 0.7 all_to_all.14
  269.2 25.6 %all-to-all-start.2 = ((f32[32,1,6]{2,1,0:T(1,128)}), f32[32,1,6]{2,1,0:T(1,128)S(1)}, u32[]{:S(2)}, u32[]{:S(2)}) async-start(f32[32,1,6]{2,1,0:T(1,128)} %bitcast.32), calls=%async_computation.3 | async-start | bytes 32768 | tf_op jit(solution)/shard_map/all_to_all | solution.py:148
  294.8 0.9 pad_maximum_fusion
  295.7 21.7 %all-to-all-done.2 = f32[32,1,6]{2,1,0:T(1,128)S(1)} async-done(((f32[32,1,6]{2,1,0:T(1,128)}), f32[32,1,6]{2,1,0:T(1,128)S(1)}, u32[]{:S(2)}, u32[]{:S(2)}) %all-to-all-start.2) | async-done | bytes 800 | tf_op jit(solution)/shard_map/all_to_all | solution.py:148
  317.4 0.5 broadcast.32
  317.9 0.7 reduce.5
  318.6 0.1 broadcast_in_dim.24
  318.7 0.6 select_reduce_fusion
  319.3 22.0 %reduce-scatter.2.cloned.1.call-done = f32[128,768]{1,0:T(8,128)} async-done(((f32[1024,768]{1,0:T(8,128)}), f32[128,768]{1,0:T(8,128)}) %reduce-scatter.2.cloned.1.call-update) | async-done | bytes 393232 | tf_op jit(solution)/shard_map/reduce_scatter | solution.py:134
  341.3 1.7 convert_bitcast_fusion
  (35 shorter events, 0.3 us)
Async XLA Ops:
  7.2 1.2 copy-start.1
  8.4 0.7 copy-start.2
  9.0 0.7 copy-start.3
  13.5 37.3 %copy-start.5 = (bf16[1,1,192,1536]{3,2,1,0:T(8,128)(2,1)S(1)}, bf16[1,1,192,1536]{3,2,1,0:T(8,128)(2,1)}, u32[]{:S(2)}) copy-start(bf16[1,1,192,1536]{3,2,1,0:T(8,128)(2,1)} %param.9) | copy-start | bytes 1769476
  13.5 223.1 %all-to-all-start = ((bf16[128,48,128]{2,1,0:T(8,128)(2,1)}), bf16[128,48,128]{2,1,0:T(8,128)(2,1)S(1)}, u32[]{:S(2)}, u32[]{:S(2)}) async-start(bf16[128,48,128]{2,1,0:T(8,128)(2,1)} %bitcast.2), calls=%async_computation | async-start | bytes 3145728 | tf_op jit(solution)/shard_map/all_to_all | solution.py:117
  48.6 188.0 %all-gather.2.cloned.1.call-start = ((), (), s32[]{:S(2)}) async-start(), calls=%async_computation.4 | async-start | bytes 1720320 | tf_op jit(solution)/shard_map/all_gather | solution.py:131
  48.7 3.1 collective-permute-start
  51.9 9.9 %collective-permute-start.1 = (bf16[2,4,8,128]{3,2,0,1:T(8,128)(2,1)S(1)}, bf16[2,4,8,128]{3,2,0,1:T(8,128)(2,1)S(1)}, u32[]{:S(2)}, u32[]{:S(2)}) collective-permute-start(bf16[2,4,8,128]{3,2,0,1:T(8,128)(2,1)S(1)} %bitcast.81), channel_id=1, source_target_pairs={{0,6},{2,0},{4,2},{6,4},{1,7},{3,1},{5,3},{7,5},{8,14},{10,8},{12,... | collective-permute-start | bytes 49160 | tf_op jit(solution)/shard_map/ppermute | solution.py:110
  54.6 7.1 %collective-permute-start.2 = (bf16[2,4,8,128]{3,2,0,1:T(8,128)(2,1)S(1)}, bf16[2,4,8,128]{3,2,0,1:T(8,128)(2,1)S(1)}, u32[]{:S(2)}, u32[]{:S(2)}) collective-permute-start(bf16[2,4,8,128]{3,2,0,1:T(8,128)(2,1)S(1)} %bitcast.82), channel_id=1, source_target_pairs={{0,4},{2,6},{4,0},{6,2},{1,5},{3,7},{5,1},{7,3},{8,12},{10,14},{12... | collective-permute-start | bytes 49160 | tf_op jit(solution)/shard_map/ppermute | solution.py:110
  58.1 5.6 %collective-permute-start.3 = (bf16[2,4,8,128]{3,2,0,1:T(8,128)(2,1)S(1)}, bf16[2,4,8,128]{3,2,0,1:T(8,128)(2,1)S(1)}, u32[]{:S(2)}, u32[]{:S(2)}) collective-permute-start(bf16[2,4,8,128]{3,2,0,1:T(8,128)(2,1)S(1)} %bitcast.83), channel_id=1, source_target_pairs={{0,2},{2,4},{4,6},{6,0},{1,3},{3,5},{5,7},{7,1},{8,10},{10,12},{12... | collective-permute-start | bytes 49160 | tf_op jit(solution)/shard_map/ppermute | solution.py:110
  63.8 132.0 %collective-permute-start.4 = (bf16[4,2,8,128]{3,2,1,0:T(8,128)(2,1)S(1)}, bf16[4,2,8,128]{3,2,1,0:T(8,128)(2,1)S(1)}, u32[]{:S(2)}, u32[]{:S(2)}) collective-permute-start(bf16[4,2,8,128]{3,2,1,0:T(8,128)(2,1)S(1)} %get-tuple-element.16), channel_id=1, source_target_pairs={{0,24},{8,0},{16,8},{24,16},{1,25},{9,1},{17,9},{25,17},{2,26},{10... | collective-permute-start | bytes 49160 | tf_op jit(solution)/shard_map/ppermute | solution.py:110
  75.7 120.1 %collective-permute-start.5 = (bf16[4,2,8,128]{3,2,1,0:T(8,128)(2,1)S(1)}, bf16[4,2,8,128]{3,2,1,0:T(8,128)(2,1)S(1)}, u32[]{:S(2)}, u32[]{:S(2)}) collective-permute-start(bf16[4,2,8,128]{3,2,1,0:T(8,128)(2,1)S(1)} %get-tuple-element.15), channel_id=1, source_target_pairs={{0,16},{8,24},{16,0},{24,8},{1,17},{9,25},{17,1},{25,9},{2,18},{10... | collective-permute-start | bytes 49160 | tf_op jit(solution)/shard_map/ppermute | solution.py:110
  87.8 108.0 %collective-permute-start.6 = (bf16[4,2,8,128]{3,2,1,0:T(8,128)(2,1)S(1)}, bf16[4,2,8,128]{3,2,1,0:T(8,128)(2,1)S(1)}, u32[]{:S(2)}, u32[]{:S(2)}) collective-permute-start(bf16[4,2,8,128]{3,2,1,0:T(8,128)(2,1)S(1)} %get-tuple-element.14), channel_id=1, source_target_pairs={{0,8},{8,16},{16,24},{24,0},{1,9},{9,17},{17,25},{25,1},{2,10},{10... | collective-permute-start | bytes 49160 | tf_op jit(solution)/shard_map/ppermute | solution.py:110
  196.7 144.6 %reduce-scatter.2.cloned.1.call-start = ((), (), s32[]{:S(2)}) async-start(), calls=%async_computation.5 | async-start | bytes 3538944 | tf_op jit(solution)/shard_map/reduce_scatter | solution.py:134
  236.5 1.3 copy-start
  248.1 3.7 %copy-start.4 = (s32[128,1]{0,1:T(1,128)S(1)}, s32[128,1]{0,1:T(1,128)}, u32[]{:S(2)}) copy-start(s32[128,1]{0,1:T(1,128)} %param.6) | copy-start | bytes 1540
  248.1 19.9 %copy-start.6 = (bf16[1,1,192,1536]{3,2,1,0:T(8,128)(2,1)S(1)}, bf16[1,1,192,1536]{3,2,1,0:T(8,128)(2,1)}, u32[]{:S(2)}) copy-start(bf16[1,1,192,1536]{3,2,1,0:T(8,128)(2,1)} %param.9) | copy-start | bytes 1769476
  248.1 19.7 %all-to-all-start.1 = ((bf16[4,192,768]{2,1,0:T(8,128)(2,1)}), bf16[4,192,768]{2,1,0:T(8,128)(2,1)S(1)}, u32[]{:S(2)}, u32[]{:S(2)}) async-start(bf16[4,192,768]{2,1,0:T(8,128)(2,1)} %bitcast.78), calls=%async_computation.2 | async-start | bytes 2359296 | tf_op jit(solution)/shard_map/all_to_all | solution.py:139
  269.2 48.2 %all-to-all-start.2 = ((f32[32,1,6]{2,1,0:T(1,128)}), f32[32,1,6]{2,1,0:T(1,128)S(1)}, u32[]{:S(2)}, u32[]{:S(2)}) async-start(f32[32,1,6]{2,1,0:T(1,128)} %bitcast.32), calls=%async_computation.3 | async-start | bytes 32768 | tf_op jit(solution)/shard_map/all_to_all | solution.py:148
Sparse Core Ops, SparseCore 0:
  196.9 39.6 all-gather.1
  244.3 96.9 reduce-scatter.1

commit v2 on v1

v2 whole, which is shorter than its diff:
```python
import jax
import jax.numpy as jnp
from jax import lax
from jax.experimental import pallas as pl
from jax.experimental.pallas import tpu as pltpu
from jax.sharding import Mesh
from jax.sharding import PartitionSpec as P

BF16, F32, I32 = jnp.bfloat16, jnp.float32, jnp.int32
ZL, X, ZH, Y, C = 8, 4, 4, 4, 2
E = ZH * Y * C
CAP = 6
TOK = 128
FFW = 768
LANES = 128
EXPERT = ("zh", "y", "c")
BLOCK = ZL * CAP
FAN = X * E
SLOTS = E * CAP
ROWS = X * SLOTS
WIDE = ZL * LANES
SUB = 16
VMEM = 24 * 1024 * 1024


def pack_kernel(ids_ref, gate_ref, grad_ref, rows_ref, keys, gates, grads):
    ids = ids_ref[...]
    onehot = (lax.broadcasted_iota(I32, (E, TOK), 0) == ids).astype(F32)
    earlier = lax.broadcasted_iota(I32, (TOK, TOK), 0) < lax.broadcasted_iota(I32, (TOK, TOK), 1)
    before = jnp.dot(onehot.astype(BF16), earlier.astype(BF16), preferred_element_type=F32)
    place = jnp.sum(before * onehot, axis=0, keepdims=True).astype(I32)
    base = ids * BLOCK + place
    for z in range(ZL):
        keys[:, z * TOK : (z + 1) * TOK] = base + z * CAP
        gates[:, z * TOK : (z + 1) * TOK] = gate_ref[...].astype(F32)
        grads[z * TOK : (z + 1) * TOK, :] = grad_ref[:, z * (X * LANES) : (z + 1) * (X * LANES)]
    step = 8 * BLOCK

    def body(i, carry):
        row = lax.broadcasted_iota(I32, (step, ZL * TOK), 0) + i * step
        take = jnp.where(row == keys[...], gates[...], 0.0).astype(BF16)
        out = jnp.dot(take, grads[...], preferred_element_type=F32).astype(BF16)
        for q in range(X):
            rows_ref[q, pl.ds(pl.multiple_of(i * step, step), step), :] = out[:, q * LANES : (q + 1) * LANES]
        return carry

    lax.fori_loop(0, E * BLOCK // step, body, 0)


def pack(ids, gates, grad):
    return pl.pallas_call(
        pack_kernel,
        out_shape=jax.ShapeDtypeStruct((X, E * BLOCK, LANES), BF16),
        scratch_shapes=[
            pltpu.VMEM((1, ZL * TOK), I32),
            pltpu.VMEM((1, ZL * TOK), F32),
            pltpu.VMEM((ZL * TOK, X * LANES), BF16),
        ],
        compiler_params=pltpu.CompilerParams(vmem_limit_bytes=VMEM),
        cost_estimate=pl.CostEstimate(flops=2 * E * BLOCK * ZL * TOK * X * LANES, bytes_accessed=3 << 20, transcendentals=0),
        name="pack",
    )(ids, gates, grad)


def weight_kernel(recv_ref, acts_ref, *outs):
    part_ref, scaled_ref = outs
    size = SUB * BLOCK
    group = SUB * CAP
    out = lax.broadcasted_iota(I32, (size, size), 0)
    col = lax.broadcasted_iota(I32, (size, size), 1)
    inner = out % group
    source = (inner // CAP) * BLOCK + (out // group) * CAP + inner % CAP
    order = jnp.where(source == col, 1.0, 0.0).astype(BF16)
    for k in range(FAN // SUB):
        rows = jnp.dot(order, recv_ref[k], preferred_element_type=F32).astype(BF16)
        for z in range(ZL):
            at = z * LANES
            scaled_ref[k * group : (k + 1) * group, at : at + LANES] = rows[z * group : (z + 1) * group, :]
    part_ref[...] = lax.dot_general(
        scaled_ref[...], acts_ref[...], (((0,), (0,)), ((), ())), preferred_element_type=F32
    ).astype(BF16)


def weight_part(recv, acts):
    return pl.pallas_call(
        weight_kernel,
        out_shape=(
            jax.ShapeDtypeStruct((WIDE, FFW), BF16),
            jax.ShapeDtypeStruct((ROWS, WIDE), BF16),
        ),
        compiler_params=pltpu.CompilerParams(vmem_limit_bytes=VMEM),
        cost_estimate=pl.CostEstimate(flops=4 * ROWS * ROWS * WIDE, bytes_accessed=6 << 20, transcendentals=0),
        name="weight_part",
    )(recv, acts)


def act_kernel(own_ref, scaled_ref, weight_ref, acts_ref, *outs):
    parts, score_ref, grad = outs[:X], outs[X], outs[X + 1]
    grad[...] = jnp.dot(scaled_ref[...], weight_ref[...], preferred_element_type=F32)
    for d in range(X):
        at = pl.multiple_of(lax.rem(own_ref[0] + d, X) * SLOTS, SLOTS)
        parts[d][...] = grad[pl.ds(at, SLOTS), :].astype(BF16)
    narrow = jnp.zeros((ROWS, LANES), F32)
    for f in range(0, FFW, LANES):
        narrow = narrow + grad[:, f : f + LANES] * acts_ref[:, f : f + LANES].astype(F32)
    score_ref[...] = jnp.sum(narrow.T, axis=0, keepdims=True)


def act_part(own, scaled, weight, acts):
    vmem = pl.BlockSpec(memory_space=pltpu.VMEM)
    return pl.pallas_call(
        act_kernel,
        in_specs=[pl.BlockSpec(memory_space=pltpu.SMEM), vmem, vmem, vmem],
        out_shape=[jax.ShapeDtypeStruct((SLOTS, FFW), BF16)] * X + [jax.ShapeDtypeStruct((1, ROWS), F32)],
        scratch_shapes=[pltpu.VMEM((ROWS, FFW), F32)],
        compiler_params=pltpu.CompilerParams(vmem_limit_bytes=VMEM),
        cost_estimate=pl.CostEstimate(flops=2 * ROWS * FFW * WIDE, bytes_accessed=6 << 20, transcendentals=0),
        name="act_part",
    )(own, scaled, weight, acts)


def shift(block, axis, n, d):
    return lax.ppermute(block, axis, [(i, (i + d) % n) for i in range(n)])


def per_device(out_grad, expert_ids, gate_values, down_weight, gate_up):
    own_x = lax.axis_index("x")
    rows = pack(expert_ids.reshape(1, TOK), gate_values.reshape(1, TOK), out_grad)
    recv = lax.all_to_all(
        rows.reshape(FAN, BLOCK, LANES), ("x",) + EXPERT, split_axis=0, concat_axis=0, tiled=True
    )

    saved = gate_up[0, 0]
    gate_act = saved[:, :FFW].astype(F32)
    up_act = saved[:, FFW:].astype(F32)
    sigmoid_val = jax.nn.sigmoid(gate_act)
    silu_val = gate_act * sigmoid_val
    hidden = (silu_val * up_act).astype(BF16)
    weight = lax.dynamic_index_in_dim(down_weight.reshape(ZL, X, LANES, FFW), own_x, 1, keepdims=False)
    weight = weight.reshape(WIDE, FFW)
    chosen = expert_ids.reshape(TOK)
    onehot = (chosen[:, None] == jnp.arange(E, dtype=I32)[None, :]).astype(F32)
    later = jnp.arange(TOK)[:, None] > jnp.arange(TOK)[None, :]
    before = jnp.dot(later.astype(BF16), onehot.astype(BF16), preferred_element_type=F32)
    slots = chosen * CAP + jnp.sum(before * onehot, axis=1).astype(I32)
    hidden, weight, slots = lax.optimization_barrier((hidden, weight, slots))
    came = [hidden] + [shift(hidden, "x", X, d) for d in range(1, X)]
    turned = [came[-k % X] for k in range(X)]
    acts = lax.dynamic_slice_in_dim(jnp.concatenate(turned + turned), (X - own_x) % X * SLOTS, ROWS, 0)

    part, scaled = weight_part(recv.reshape(FAN // SUB, SUB * BLOCK, LANES), acts)
    weight_share = lax.psum_scatter(part, "zl", scatter_dimension=0, tiled=True)

    *parts, score = act_part(own_x.reshape(1), scaled, weight, acts)
    returned = lax.all_to_all(
        score.reshape(FAN, 1, CAP), ("x",) + EXPERT, split_axis=0, concat_axis=0, tiled=True
    )
    hidden_grad = parts[0].astype(F32)
    for d in range(1, X):
        hidden_grad = hidden_grad + shift(parts[d], "x", X, d).astype(F32)
    gate_part = hidden_grad * up_act * sigmoid_val * (1.0 + gate_act * (1.0 - sigmoid_val))
    up_part = hidden_grad * silu_val
    gu_grad = jnp.concatenate([gate_part, up_part], axis=1).astype(BF16)

    returned = jnp.sum(returned.reshape(X, SLOTS), axis=0)
    hit = slots[:, None] == jnp.arange(SLOTS, dtype=I32)[None, :]
    route = jnp.sum(jnp.where(hit, returned[None, :], 0.0), axis=1)
    route_grad = route.reshape(TOK, 1) / gate_values.astype(F32)
    return (weight_share[None], gu_grad[None, None], route_grad)


def solution(mesh):
    fine = Mesh(mesh.devices.reshape(ZL, X, ZH, Y, C), ("zl", "x", "zh", "y", "c"))
    dp = ("zl", "x")
    return jax.shard_map(
        per_device,
        mesh=fine,
        in_specs=(
            P(dp + EXPERT, None),
            P(dp + EXPERT, None),
            P(dp + EXPERT, None),
            P(EXPERT, None, None),
            P(dp, EXPERT, None, None),
        ),
        out_specs=(
            P(EXPERT, dp, None),
            P(dp, EXPERT, None, None),
            P(dp + EXPERT, None),
        ),
        check_vma=False,
    )
```

time: 351 us -> 287 us (0.82)
  waiting for transfers between devices: 198 us -> 153 us
  starting transfers between devices: 113 us -> 77.8 us
  local copies, waits for them, and re-layouts: 6.99 us -> 24.6 us
    all_to_all x1, waiting for transfers between devices: 0.01 us -> 104 us  [per_device(): lax.all_to_all(rows.reshape(FAN, BLOCK, LANES), ('x',) + EXPERT, split_ax...]
    ppermute x7 -> x6, waiting for transfers between devices: 98.5 us -> 12.6 us  [shift(): return lax.ppermute(block, axis, [(i, (i + d) % n) for i in range(n)])]
    all_gather x1 -> x0, waiting for transfers between devices: 39.8 us -> none  [per_device(): lax.all_gather(jnp.concatenate([hidden, gate_slots], axis=1), 'x', axis=0...]
    ppermute x7 -> x6, starting transfers between devices: 48 us -> 22.2 us  [shift(): return lax.ppermute(block, axis, [(i, (i + d) % n) for i in range(n)])]
    all_to_all x2 -> x1, waiting for transfers between devices: 37.4 us -> 14.5 us  [per_device(): lax.all_to_all(score.reshape(FAN, 1, CAP), ('x',) + EXPERT, split_axis=0,...]
    unnamed x28 -> x27, local copies, waits for them, and re-layouts: 4.01 us -> 17.6 us
    all_to_all x2 -> x1, starting transfers between devices: 29.3 us -> 20.5 us  [per_device(): lax.all_to_all(score.reshape(FAN, 1, CAP), ('x',) + EXPERT, split_axis=0,...]
    pallas_call x2 -> x3, Pallas kernels: 10 us -> 11.1 us  [the longest x1 5.78 us: weight_part(): pl.pallas_call(weight_kernel, out_shape=(jax.ShapeDtypeStruct((WIDE, FFW)...]
  transfers between devices with their start and end apart: 12 -> 9, of which waited for: 7 -> 5; matrix products, arithmetic and copies ran while one was open for 3% -> 7% of each run, Pallas kernels for 0% -> 1%
where the time goes in v2:
time: 287 us; the launch traced here: 285 us
  waiting for transfers between devices  153 us (53%)
  starting transfers between devices  77.8 us (27%)
  local copies, waits for them, and re-layouts  24.6 us (9%)
  between operations  14.2 us (5%)
  Pallas kernels  11.1 us (4%)
  other arithmetic  4 us (1%)
    all_to_all x1, waiting for transfers between devices, per_device(): lax.all_to_all(rows.reshape(FAN, BLOCK, LANES), ('x',) + EXPERT, split_ax...  104 us
    all_to_all x1, starting transfers between devices, per_device(): lax.all_to_all(rows.reshape(FAN, BLOCK, LANES), ('x',) + EXPERT, split_ax...  35.1 us
    ppermute x6, starting transfers between devices, shift(): return lax.ppermute(block, axis, [(i, (i + d) % n) for i in range(n)])  22.2 us
    reduce_scatter x1, waiting for transfers between devices, per_device(): weight_share = lax.psum_scatter(part, 'zl', scatter_dimension=0, tiled=True)  22 us
    all_to_all x1, starting transfers between devices, per_device(): lax.all_to_all(score.reshape(FAN, 1, CAP), ('x',) + EXPERT, split_axis=0,...  20.5 us
    unnamed x27, local copies, waits for them, and re-layouts  17.6 us
    all_to_all x1, waiting for transfers between devices, per_device(): lax.all_to_all(score.reshape(FAN, 1, CAP), ('x',) + EXPERT, split_axis=0,...  14.5 us
    ppermute x6, waiting for transfers between devices, shift(): return lax.ppermute(block, axis, [(i, (i + d) % n) for i in range(n)])  12.6 us
  transfers between devices with their start and end apart: 9, of which 5 were waited for; matrix products, arithmetic and copies ran while one was open for 7% of the time, Pallas kernels for 1%

profile of v2, /device:TPU:24, one launch (start us, length us, event | category | flops | bytes accessed | tf_op | source)
XLA Modules:
  0.0 284.9 jit_solution(15418195890625701531)
XLA Ops:
  7.2 1.2 copy-done.2
  8.4 0.7 copy-done.3
  9.0 0.7 copy-done.5
  9.7 3.6 %pack.1 = bf16[4,1536,128]{2,1,0:T(8,128)(2,1)} custom-call(s32[1,128]{1,0:T(1,128)S(1)} %bitcast.22, bf16[1,128]{1,0:T(2,128)(2,1)S(1)} %bitcast.24, bf16[128,4096]{1,0:T(8,128)(2,1)S(1)} %copy-done.2), custom_call_target="tpu_custom_call" | custom-call | flops 1610612736 | bytes 3145728 | tf_op jit(solution)/shard_map/pack/pallas_call | solution.py:51
  13.3 35.1 %all-to-all-start = ((bf16[128,48,128]{2,1,0:T(8,128)(2,1)}), bf16[128,48,128]{2,1,0:T(8,128)(2,1)S(1)}, u32[]{:S(2)}, u32[]{:S(2)}) async-start(bf16[128,48,128]{2,1,0:T(8,128)(2,1)} %bitcast.2), calls=%async_computation | async-start | bytes 3145728 | tf_op jit(solution)/shard_map/all_to_all | solution.py:129
  48.4 0.0 reduce-scatter.2.cloned.1.call-start
  48.5 0.2 fusion
  48.7 1.5 constant_dynamic-slice_fusion.1
  50.2 1.2 fusion.1
  51.4 5.2 %collective-permute-start = (bf16[192,768]{1,0:T(8,128)(2,1)S(1)}, bf16[192,768]{1,0:T(8,128)(2,1)}, u32[]{:S(2)}, u32[]{:S(2)}) collective-permute-start(bf16[192,768]{1,0:T(8,128)(2,1)S(1)} %fusion.1), channel_id=1, source_target_pairs={{0,96},{32,0},{64,32},{96,64},{1,97},{33,1},{65,33},{97,65},{2,98}... | collective-permute-start | bytes 884744 | tf_op jit(solution)/shard_map/ppermute | solution.py:123
  56.6 2.3 collective-permute-start.1
  58.9 3.0 %collective-permute-start.2 = (bf16[192,768]{1,0:T(8,128)(2,1)S(1)}, bf16[192,768]{1,0:T(8,128)(2,1)}, u32[]{:S(2)}, u32[]{:S(2)}) collective-permute-start(bf16[192,768]{1,0:T(8,128)(2,1)S(1)} %fusion.1), channel_id=1, source_target_pairs={{0,32},{32,64},{64,96},{96,0},{1,33},{33,65},{65,97},{97,1},{2,34}... | collective-permute-start | bytes 884744 | tf_op jit(solution)/shard_map/ppermute | solution.py:123
  61.9 0.7 constant_dynamic-update-slice_fusion.7
  62.7 10.1 %collective-permute-done = bf16[192,768]{1,0:T(8,128)(2,1)} collective-permute-done((bf16[192,768]{1,0:T(8,128)(2,1)S(1)}, bf16[192,768]{1,0:T(8,128)(2,1)}, u32[]{:S(2)}, u32[]{:S(2)}) %collective-permute-start) | collective-permute-done | bytes 294944 | tf_op jit(solution)/shard_map/ppermute | solution.py:123
  72.7 1.7 constant_dynamic-update-slice_fusion.6
  74.4 0.0 collective-permute-done.1
  74.4 1.7 constant_dynamic-update-slice_fusion.5
  76.1 2.5 collective-permute-done.2
  78.6 1.7 constant_dynamic-update-slice_fusion.4
  80.3 0.7 constant_dynamic-update-slice_fusion.3
  81.1 1.7 constant_dynamic-update-slice_fusion.2
  82.8 1.7 constant_dynamic-update-slice_fusion.1
  84.5 1.7 constant_dynamic-update-slice_fusion
  86.2 2.4 constant_dynamic-slice_fusion.acts_ref
  88.5 104.1 %all-to-all-done = bf16[128,48,128]{2,1,0:T(8,128)(2,1)S(1)} async-done(((bf16[128,48,128]{2,1,0:T(8,128)(2,1)}), bf16[128,48,128]{2,1,0:T(8,128)(2,1)S(1)}, u32[]{:S(2)}, u32[]{:S(2)}) %all-to-all-start) | async-done | bytes 1572896 | tf_op jit(solution)/shard_map/all_to_all | solution.py:129
  192.6 1.3 copy-done
  193.9 5.8 %weight_part.1 = (bf16[1024,768]{1,0:T(8,128)(2,1)}, bf16[768,1024]{1,0:T(8,128)(2,1)S(1)}) custom-call(bf16[8,768,128]{2,1,0:T(8,128)(2,1)S(1)} %bitcast.20, bf16[768,768]{1,0:T(8,128)(2,1)S(1)} %copy-done), custom_call_target="tpu_custom_call" | custom-call | flops 2415919104 | bytes 6291456 | tf_op jit(solution)/shard_map/weight_part/pallas_call | solution.py:85
  199.7 1.1 copy-done.7
  200.8 0.0 reduce-scatter.2.cloned.1.call-update
  200.9 1.3 copy-done.1
  202.1 1.4 copy-done.8
  203.5 1.7 act_part.1
  205.3 0.8 reshape.81
  206.1 20.5 %all-to-all-start.1 = ((f32[128,1,6]{2,1,0:T(1,128)}), f32[128,1,6]{2,1,0:T(1,128)S(1)}, u32[]{:S(2)}, u32[]{:S(2)}) async-start(f32[128,1,6]{2,1,0:T(1,128)} %bitcast.12), calls=%async_computation.2 | async-start | bytes 131072 | tf_op jit(solution)/shard_map/all_to_all | solution.py:155
  226.5 3.5 %collective-permute-start.3 = (bf16[192,768]{1,0:T(8,128)(2,1)S(1)}, bf16[192,768]{1,0:T(8,128)(2,1)S(1)}, u32[]{:S(2)}, u32[]{:S(2)}) collective-permute-start(bf16[192,768]{1,0:T(8,128)(2,1)S(1)} %get-tuple-element.18), channel_id=1, source_target_pairs={{0,32},{32,64},{64,96},{96,0},{1,33},{33,65},{65,97},{97,1},{2,34}... | collective-permute-start | bytes 884744 | tf_op jit(solution)/shard_map/ppermute | solution.py:123
  230.1 5.0 %collective-permute-start.4 = (bf16[192,768]{1,0:T(8,128)(2,1)S(1)}, bf16[192,768]{1,0:T(8,128)(2,1)S(1)}, u32[]{:S(2)}, u32[]{:S(2)}) collective-permute-start(bf16[192,768]{1,0:T(8,128)(2,1)S(1)} %get-tuple-element.19), channel_id=1, source_target_pairs={{0,64},{32,96},{64,0},{96,32},{1,65},{33,97},{65,1},{97,33},{2,66}... | collective-permute-start | bytes 884744 | tf_op jit(solution)/shard_map/ppermute | solution.py:123
  235.1 3.2 %collective-permute-start.5 = (bf16[192,768]{1,0:T(8,128)(2,1)S(1)}, bf16[192,768]{1,0:T(8,128)(2,1)S(1)}, u32[]{:S(2)}, u32[]{:S(2)}) collective-permute-start(bf16[192,768]{1,0:T(8,128)(2,1)S(1)} %get-tuple-element.20), channel_id=1, source_target_pairs={{0,96},{32,0},{64,32},{96,64},{1,97},{33,1},{65,33},{97,65},{2,98}... | collective-permute-start | bytes 884744 | tf_op jit(solution)/shard_map/ppermute | solution.py:123
  238.2 14.5 %all-to-all-done.1 = f32[128,1,6]{2,1,0:T(1,128)S(1)} async-done(((f32[128,1,6]{2,1,0:T(1,128)}), f32[128,1,6]{2,1,0:T(1,128)S(1)}, u32[]{:S(2)}, u32[]{:S(2)}) %all-to-all-start.1) | async-done | bytes 3104 | tf_op jit(solution)/shard_map/all_to_all | solution.py:155
  252.7 0.5 broadcast.24
  253.2 0.8 reduce.4
  254.0 0.1 reshape.82
  254.2 0.1 select_reduce_fusion
  254.3 0.5 bitcast_divide_fusion
  254.8 0.0 collective-permute-done.3
  254.8 0.0 collective-permute-done.4
  254.8 0.4 fusion.10
  255.3 0.9 pad_maximum_fusion
  256.1 22.0 %reduce-scatter.2.cloned.1.call-done = bf16[128,768]{1,0:T(8,128)(2,1)} async-done(((bf16[1024,768]{1,0:T(8,128)(2,1)}), bf16[128,768]{1,0:T(8,128)(2,1)}) %reduce-scatter.2.cloned.1.call-update) | async-done | bytes 196624 | tf_op jit(solution)/shard_map/reduce_scatter | solution.py:152
  (17 shorter events, 0.1 us)
Async XLA Ops:
  7.2 1.2 copy-start.2
  8.4 0.7 copy-start.3
  9.0 0.7 copy-start.5
  13.3 35.2 %copy-start.4 = (s32[128,1]{0,1:T(1,128)S(1)}, s32[128,1]{0,1:T(1,128)}, u32[]{:S(2)}) copy-start(s32[128,1]{0,1:T(1,128)} %param.6) | copy-start | bytes 1540
  13.3 179.3 %all-to-all-start = ((bf16[128,48,128]{2,1,0:T(8,128)(2,1)}), bf16[128,48,128]{2,1,0:T(8,128)(2,1)S(1)}, u32[]{:S(2)}, u32[]{:S(2)}) async-start(bf16[128,48,128]{2,1,0:T(8,128)(2,1)} %bitcast.2), calls=%async_computation | async-start | bytes 3145728 | tf_op jit(solution)/shard_map/all_to_all | solution.py:129
  48.4 229.7 %reduce-scatter.2.cloned.1.call-start = ((), (), s32[]{:S(2)}) async-start(), calls=%async_computation.3 | async-start | bytes 1769472 | tf_op jit(solution)/shard_map/reduce_scatter | solution.py:152
  51.4 21.3 %collective-permute-start = (bf16[192,768]{1,0:T(8,128)(2,1)S(1)}, bf16[192,768]{1,0:T(8,128)(2,1)}, u32[]{:S(2)}, u32[]{:S(2)}) collective-permute-start(bf16[192,768]{1,0:T(8,128)(2,1)S(1)} %fusion.1), channel_id=1, source_target_pairs={{0,96},{32,0},{64,32},{96,64},{1,97},{33,1},{65,33},{97,65},{2,98}... | collective-permute-start | bytes 884744 | tf_op jit(solution)/shard_map/ppermute | solution.py:123
  56.6 17.8 %collective-permute-start.1 = (bf16[192,768]{1,0:T(8,128)(2,1)S(1)}, bf16[192,768]{1,0:T(8,128)(2,1)}, u32[]{:S(2)}, u32[]{:S(2)}) collective-permute-start(bf16[192,768]{1,0:T(8,128)(2,1)S(1)} %fusion.1), channel_id=1, source_target_pairs={{0,64},{32,96},{64,0},{96,32},{1,65},{33,97},{65,1},{97,33},{2,66}... | collective-permute-start | bytes 884744 | tf_op jit(solution)/shard_map/ppermute | solution.py:123
  58.9 19.7 %collective-permute-start.2 = (bf16[192,768]{1,0:T(8,128)(2,1)S(1)}, bf16[192,768]{1,0:T(8,128)(2,1)}, u32[]{:S(2)}, u32[]{:S(2)}) collective-permute-start(bf16[192,768]{1,0:T(8,128)(2,1)S(1)} %fusion.1), channel_id=1, source_target_pairs={{0,32},{32,64},{64,96},{96,0},{1,33},{33,65},{65,97},{97,1},{2,34}... | collective-permute-start | bytes 884744 | tf_op jit(solution)/shard_map/ppermute | solution.py:123
  192.6 1.3 copy-start
  199.7 1.2 copy-start.7
  200.9 1.3 copy-start.1
  202.1 1.4 copy-start.8
  203.5 50.7 %copy-start.6 = (bf16[128,1]{0,1:T(2,128)(2,1)S(1)}, bf16[128,1]{0,1:T(2,128)(2,1)}, u32[]{:S(2)}) copy-start(bf16[128,1]{0,1:T(2,128)(2,1)} %param.7) | copy-start | bytes 772
  203.5 51.3 %copy-start.9 = (bf16[1,1,192,1536]{3,2,1,0:T(8,128)(2,1)S(1)}, bf16[1,1,192,1536]{3,2,1,0:T(8,128)(2,1)}, u32[]{:S(2)}) copy-start(bf16[1,1,192,1536]{3,2,1,0:T(8,128)(2,1)} %param.9) | copy-start | bytes 1769476
  206.1 46.6 %all-to-all-start.1 = ((f32[128,1,6]{2,1,0:T(1,128)}), f32[128,1,6]{2,1,0:T(1,128)S(1)}, u32[]{:S(2)}, u32[]{:S(2)}) async-start(f32[128,1,6]{2,1,0:T(1,128)} %bitcast.12), calls=%async_computation.2 | async-start | bytes 131072 | tf_op jit(solution)/shard_map/all_to_all | solution.py:155
  226.5 28.3 %collective-permute-start.3 = (bf16[192,768]{1,0:T(8,128)(2,1)S(1)}, bf16[192,768]{1,0:T(8,128)(2,1)S(1)}, u32[]{:S(2)}, u32[]{:S(2)}) collective-permute-start(bf16[192,768]{1,0:T(8,128)(2,1)S(1)} %get-tuple-element.18), channel_id=1, source_target_pairs={{0,32},{32,64},{64,96},{96,0},{1,33},{33,65},{65,97},{97,1},{2,34}... | collective-permute-start | bytes 884744 | tf_op jit(solution)/shard_map/ppermute | solution.py:123
  230.1 24.8 %collective-permute-start.4 = (bf16[192,768]{1,0:T(8,128)(2,1)S(1)}, bf16[192,768]{1,0:T(8,128)(2,1)S(1)}, u32[]{:S(2)}, u32[]{:S(2)}) collective-permute-start(bf16[192,768]{1,0:T(8,128)(2,1)S(1)} %get-tuple-element.19), channel_id=1, source_target_pairs={{0,64},{32,96},{64,0},{96,32},{1,65},{33,97},{65,1},{97,33},{2,66}... | collective-permute-start | bytes 884744 | tf_op jit(solution)/shard_map/ppermute | solution.py:123
  235.1 19.7 %collective-permute-start.5 = (bf16[192,768]{1,0:T(8,128)(2,1)S(1)}, bf16[192,768]{1,0:T(8,128)(2,1)S(1)}, u32[]{:S(2)}, u32[]{:S(2)}) collective-permute-start(bf16[192,768]{1,0:T(8,128)(2,1)S(1)} %get-tuple-element.20), channel_id=1, source_target_pairs={{0,96},{32,0},{64,32},{96,64},{1,97},{33,1},{65,33},{97,65},{2,98}... | collective-permute-start | bytes 884744 | tf_op jit(solution)/shard_map/ppermute | solution.py:123
Sparse Core Ops, SparseCore 0:
  201.0 77.0 reduce-scatter.1

commit v3 on v2

--- a/solution.py
+++ b/solution.py
@@ -7,7 +7,8 @@
 from jax.sharding import PartitionSpec as P
 
 BF16, F32, I32 = jnp.bfloat16, jnp.float32, jnp.int32
-ZL, X, ZH, Y, C = 8, 4, 4, 4, 2
+ZA, ZB, X, ZH, Y, C = 2, 4, 4, 4, 4, 2
+ZL = ZA * ZB
 E = ZH * Y * C
 CAP = 6
 TOK = 128
@@ -62,8 +63,8 @@
     )(ids, gates, grad)
 
 
-def weight_kernel(recv_ref, acts_ref, *outs):
-    part_ref, scaled_ref = outs
+def weight_kernel(own_ref, recv_ref, acts_ref, *outs):
+    parts, scaled_ref = outs[:ZB], outs[ZB]
     size = SUB * BLOCK
     group = SUB * CAP
     out = lax.broadcasted_iota(I32, (size, size), 0)
@@ -74,24 +75,29 @@
     for k in range(FAN // SUB):
         rows = jnp.dot(order, recv_ref[k], preferred_element_type=F32).astype(BF16)
         for z in range(ZL):
-            at = z * LANES
+            at = ((z % ZB) * ZA + z // ZB) * LANES
             scaled_ref[k * group : (k + 1) * group, at : at + LANES] = rows[z * group : (z + 1) * group, :]
-    part_ref[...] = lax.dot_general(
-        scaled_ref[...], acts_ref[...], (((0,), (0,)), ((), ())), preferred_element_type=F32
-    ).astype(BF16)
-
-
-def weight_part(recv, acts):
+    for d in range(ZB):
+        at = pl.multiple_of(lax.rem(own_ref[0] + d, ZB) * (ZA * LANES), ZA * LANES)
+        parts[d][...] = lax.dot_general(
+            scaled_ref[:, pl.ds(at, ZA * LANES)],
+            acts_ref[...],
+            (((0,), (0,)), ((), ())),
+            preferred_element_type=F32,
+        ).astype(BF16)
+
+
+def weight_part(own, recv, acts):
+    vmem = pl.BlockSpec(memory_space=pltpu.VMEM)
     return pl.pallas_call(
         weight_kernel,
-        out_shape=(
-            jax.ShapeDtypeStruct((WIDE, FFW), BF16),
-            jax.ShapeDtypeStruct((ROWS, WIDE), BF16),
-        ),
+        in_specs=[pl.BlockSpec(memory_space=pltpu.SMEM), vmem, vmem],
+        out_shape=[jax.ShapeDtypeStruct((ZA * LANES, FFW), BF16)] * ZB
+        + [jax.ShapeDtypeStruct((ROWS, WIDE), BF16)],
         compiler_params=pltpu.CompilerParams(vmem_limit_bytes=VMEM),
         cost_estimate=pl.CostEstimate(flops=4 * ROWS * ROWS * WIDE, bytes_accessed=6 << 20, transcendentals=0),
         name="weight_part",
-    )(recv, acts)
+    )(own, recv, acts)
 
 
 def act_kernel(own_ref, scaled_ref, weight_ref, acts_ref, *outs):
@@ -124,7 +130,7 @@
 
 
 def per_device(out_grad, expert_ids, gate_values, down_weight, gate_up):
-    own_x = lax.axis_index("x")
+    own_x, own_za, own_zb = (lax.axis_index(a) for a in ("x", "za", "zb"))
     rows = pack(expert_ids.reshape(1, TOK), gate_values.reshape(1, TOK), out_grad)
     recv = lax.all_to_all(
         rows.reshape(FAN, BLOCK, LANES), ("x",) + EXPERT, split_axis=0, concat_axis=0, tiled=True
@@ -136,8 +142,8 @@
     sigmoid_val = jax.nn.sigmoid(gate_act)
     silu_val = gate_act * sigmoid_val
     hidden = (silu_val * up_act).astype(BF16)
-    weight = lax.dynamic_index_in_dim(down_weight.reshape(ZL, X, LANES, FFW), own_x, 1, keepdims=False)
-    weight = weight.reshape(WIDE, FFW)
+    weight = lax.dynamic_index_in_dim(down_weight.reshape(ZA, ZB, X, LANES, FFW), own_x, 2, keepdims=False)
+    weight = weight.swapaxes(0, 1).reshape(WIDE, FFW)
     chosen = expert_ids.reshape(TOK)
     onehot = (chosen[:, None] == jnp.arange(E, dtype=I32)[None, :]).astype(F32)
     later = jnp.arange(TOK)[:, None] > jnp.arange(TOK)[None, :]
@@ -148,10 +154,17 @@
     turned = [came[-k % X] for k in range(X)]
     acts = lax.dynamic_slice_in_dim(jnp.concatenate(turned + turned), (X - own_x) % X * SLOTS, ROWS, 0)
 
-    part, scaled = weight_part(recv.reshape(FAN // SUB, SUB * BLOCK, LANES), acts)
-    weight_share = lax.psum_scatter(part, "zl", scatter_dimension=0, tiled=True)
-
+    *sums, scaled = weight_part(own_zb.reshape(1), recv.reshape(FAN // SUB, SUB * BLOCK, LANES), acts)
+    near = [sums[0]] + [shift(sums[d], "zb", ZB, d) for d in range(1, ZB)]
     *parts, score = act_part(own_x.reshape(1), scaled, weight, acts)
+    near[1], parts, score = lax.optimization_barrier((near[1], parts, score))
+
+    near = sum(part.astype(F32) for part in near)
+    near = near.reshape(ZA, LANES, FFW)
+    away = lax.dynamic_index_in_dim(near, 1 - own_za, 0, keepdims=False).astype(BF16)
+    stay = lax.dynamic_index_in_dim(near, own_za, 0, keepdims=False)
+    weight_share = (stay + shift(away, "za", ZA, 1).astype(F32)).astype(BF16)
+
     returned = lax.all_to_all(
         score.reshape(FAN, 1, CAP), ("x",) + EXPERT, split_axis=0, concat_axis=0, tiled=True
     )
@@ -170,8 +183,8 @@
 
 
 def solution(mesh):
-    fine = Mesh(mesh.devices.reshape(ZL, X, ZH, Y, C), ("zl", "x", "zh", "y", "c"))
-    dp = ("zl", "x")
+    fine = Mesh(mesh.devices.reshape(ZA, ZB, X, ZH, Y, C), ("za", "zb", "x", "zh", "y", "c"))
+    dp = ("za", "zb", "x")
     return jax.shard_map(
         per_device,
         mesh=fine,

time: 287 us -> 281 us (0.979)
  the two profiles are of different devices: /device:TPU:24 before, /device:TPU:64 now
where the time goes in v3:
time: 281 us; the launch traced here: 280 us
  waiting for transfers between devices  129 us (46%)
  starting transfers between devices  108 us (38%)
  local copies, waits for them, and re-layouts  25.4 us (9%)
  Pallas kernels  10.4 us (4%)
  other arithmetic  6.13 us (2%)
    all_to_all x1, waiting for transfers between devices, per_device(): lax.all_to_all(rows.reshape(FAN, BLOCK, LANES), ('x',) + EXPERT, split_ax...  89.4 us
    ppermute x10, starting transfers between devices, shift(): return lax.ppermute(block, axis, [(i, (i + d) % n) for i in range(n)])  68.1 us
    all_to_all x1, starting transfers between devices, per_device(): lax.all_to_all(rows.reshape(FAN, BLOCK, LANES), ('x',) + EXPERT, split_ax...  33.9 us
    ppermute x10, waiting for transfers between devices, shift(): return lax.ppermute(block, axis, [(i, (i + d) % n) for i in range(n)])  29.3 us
    unnamed x29, local copies, waits for them, and re-layouts  18.3 us
    all_to_all x1, waiting for transfers between devices, per_device(): lax.all_to_all(score.reshape(FAN, 1, CAP), ('x',) + EXPERT, split_axis=0,...  10.2 us
    all_to_all x1, starting transfers between devices, per_device(): lax.all_to_all(score.reshape(FAN, 1, CAP), ('x',) + EXPERT, split_axis=0,...  6.15 us
  transfers between devices with their start and end apart: 12, of which 5 were waited for; matrix products, arithmetic and copies ran while one was open for 7% of the time, Pallas kernels for 1%

profile of v3, /device:TPU:64, one launch (start us, length us, event | category | flops | bytes accessed | tf_op | source)
XLA Modules:
  0.0 280.0 jit_solution(17087193624208924366)
XLA Ops:
  0.6 1.2 copy-done.2
  1.9 0.7 copy-done.3
  2.5 0.7 copy-done.5
  3.2 3.6 %pack.1 = bf16[4,1536,128]{2,1,0:T(8,128)(2,1)} custom-call(s32[1,128]{1,0:T(1,128)S(1)} %bitcast.35, bf16[1,128]{1,0:T(2,128)(2,1)S(1)} %bitcast.37, bf16[128,4096]{1,0:T(8,128)(2,1)S(1)} %copy-done.2), custom_call_target="tpu_custom_call" | custom-call | flops 1610612736 | bytes 3145728 | tf_op jit(solution)/shard_map/pack/pallas_call | solution.py:52
  6.8 33.9 %all-to-all-start = ((bf16[128,48,128]{2,1,0:T(8,128)(2,1)}), bf16[128,48,128]{2,1,0:T(8,128)(2,1)S(1)}, u32[]{:S(2)}, u32[]{:S(2)}) async-start(bf16[128,48,128]{2,1,0:T(8,128)(2,1)} %bitcast.3), calls=%async_computation | async-start | bytes 3145728 | tf_op jit(solution)/shard_map/all_to_all | solution.py:135
  40.6 1.5 constant_dynamic-slice_fusion.1
  42.3 0.5 copy-done.4
  43.0 0.3 copy-done.9
  43.2 0.2 fusion.1
  43.4 4.8 %collective-permute-start = (bf16[192,768]{1,0:T(8,128)(2,1)S(1)}, bf16[192,768]{1,0:T(8,128)(2,1)}, u32[]{:S(2)}, u32[]{:S(2)}) collective-permute-start(bf16[192,768]{1,0:T(8,128)(2,1)S(1)} %fusion.1), channel_id=1, source_target_pairs={{0,96},{32,0},{64,32},{96,64},{1,97},{33,1},{65,33},{97,65},{2,98}... | collective-permute-start | bytes 884744 | tf_op jit(solution)/shard_map/ppermute | solution.py:129
  48.2 2.3 collective-permute-start.1
  50.6 3.0 %collective-permute-start.2 = (bf16[192,768]{1,0:T(8,128)(2,1)S(1)}, bf16[192,768]{1,0:T(8,128)(2,1)}, u32[]{:S(2)}, u32[]{:S(2)}) collective-permute-start(bf16[192,768]{1,0:T(8,128)(2,1)S(1)} %fusion.1), channel_id=1, source_target_pairs={{0,32},{32,64},{64,96},{96,0},{1,33},{33,65},{65,97},{97,1},{2,34}... | collective-permute-start | bytes 884744 | tf_op jit(solution)/shard_map/ppermute | solution.py:129
  53.6 0.7 constant_dynamic-update-slice_fusion.7
  54.3 7.9 %collective-permute-done = bf16[192,768]{1,0:T(8,128)(2,1)} collective-permute-done((bf16[192,768]{1,0:T(8,128)(2,1)S(1)}, bf16[192,768]{1,0:T(8,128)(2,1)}, u32[]{:S(2)}, u32[]{:S(2)}) %collective-permute-start) | collective-permute-done | bytes 294944 | tf_op jit(solution)/shard_map/ppermute | solution.py:129
  62.2 1.7 constant_dynamic-update-slice_fusion.6
  63.9 1.7 constant_dynamic-update-slice_fusion.5
  65.5 2.2 collective-permute-done.2
  67.7 1.7 constant_dynamic-update-slice_fusion.4
  69.4 0.7 constant_dynamic-update-slice_fusion.3
  70.1 1.7 constant_dynamic-update-slice_fusion.2
  71.8 1.7 constant_dynamic-update-slice_fusion.1
  73.5 1.7 constant_dynamic-update-slice_fusion
  75.2 2.4 constant_dynamic-slice_fusion.acts_ref
  77.6 89.4 %all-to-all-done = bf16[128,48,128]{2,1,0:T(8,128)(2,1)S(1)} async-done(((bf16[128,48,128]{2,1,0:T(8,128)(2,1)}), bf16[128,48,128]{2,1,0:T(8,128)(2,1)S(1)}, u32[]{:S(2)}, u32[]{:S(2)}) %all-to-all-start) | async-done | bytes 1572896 | tf_op jit(solution)/shard_map/all_to_all | solution.py:135
  166.9 1.3 copy-done
  168.2 5.1 %weight_part.1 = (bf16[256,768]{1,0:T(8,128)(2,1)S(1)}, bf16[256,768]{1,0:T(8,128)(2,1)}, bf16[256,768]{1,0:T(8,128)(2,1)}, bf16[256,768]{1,0:T(8,128)(2,1)}, bf16[768,1024]{1,0:T(8,128)(2,1)S(1)}) custom-call(s32[1]{0:T(128)} %bitcast.own_ref, bf16[8,768,128]{2,1,0:T(8,128)(2,1)S(1)} %bitcast.34, bf16[768,768]{1,0:T(8,128)(2,1)S(1)} %copy-done), custom_call_target="tpu_custom_call" | custom-call | flops 2415919104 | bytes 6291456 | tf_op jit(solution)/shard_map/weight_part/pallas_call | solution.py:92
  173.3 1.2 copy-done.7
  174.4 35.2 %collective-permute-start.3 = (bf16[256,768]{1,0:T(8,128)(2,1)}, bf16[256,768]{1,0:T(8,128)(2,1)}, u32[]{:S(2)}, u32[]{:S(2)}) collective-permute-start(bf16[256,768]{1,0:T(8,128)(2,1)} %get-tuple-element.24), channel_id=1, source_target_pairs={{0,128},{128,256},{256,384},{384,0},{1,129},{129,257},{257,385},{3... | collective-permute-start | bytes 1179656 | tf_op jit(solution)/shard_map/ppermute | solution.py:129
  209.6 3.0 %collective-permute-start.4 = (bf16[256,768]{1,0:T(8,128)(2,1)}, bf16[256,768]{1,0:T(8,128)(2,1)}, u32[]{:S(2)}, u32[]{:S(2)}) collective-permute-start(bf16[256,768]{1,0:T(8,128)(2,1)} %get-tuple-element.33), channel_id=1, source_target_pairs={{0,256},{128,384},{256,0},{384,128},{1,257},{129,385},{257,1},{385... | collective-permute-start | bytes 1179656 | tf_op jit(solution)/shard_map/ppermute | solution.py:129
  212.7 2.3 collective-permute-start.5
  215.0 1.3 copy-done.1
  216.2 1.4 copy-done.8
  217.6 1.7 act_part.1
  219.4 19.2 %collective-permute-done.3 = bf16[256,768]{1,0:T(8,128)(2,1)} collective-permute-done((bf16[256,768]{1,0:T(8,128)(2,1)}, bf16[256,768]{1,0:T(8,128)(2,1)}, u32[]{:S(2)}, u32[]{:S(2)}) %collective-permute-start.3) | collective-permute-done | bytes 393248 | tf_op jit(solution)/shard_map/ppermute | solution.py:129
  238.6 0.8 reshape.89
  239.4 6.1 %all-to-all-start.1 = ((f32[128,1,6]{2,1,0:T(1,128)}), f32[128,1,6]{2,1,0:T(1,128)S(1)}, u32[]{:S(2)}, u32[]{:S(2)}) async-start(f32[128,1,6]{2,1,0:T(1,128)} %bitcast.18), calls=%async_computation.1 | async-start | bytes 131072 | tf_op jit(solution)/shard_map/all_to_all | solution.py:168
  245.5 3.1 %collective-permute-start.7 = (bf16[192,768]{1,0:T(8,128)(2,1)S(1)}, bf16[192,768]{1,0:T(8,128)(2,1)S(1)}, u32[]{:S(2)}, u32[]{:S(2)}) collective-permute-start(bf16[192,768]{1,0:T(8,128)(2,1)S(1)} %get-tuple-element.36), channel_id=1, source_target_pairs={{0,32},{32,64},{64,96},{96,0},{1,33},{33,65},{65,97},{97,1},{2,34}... | collective-permute-start | bytes 884744 | tf_op jit(solution)/shard_map/ppermute | solution.py:129
  248.7 5.0 %collective-permute-start.8 = (bf16[192,768]{1,0:T(8,128)(2,1)S(1)}, bf16[192,768]{1,0:T(8,128)(2,1)}, u32[]{:S(2)}, u32[]{:S(2)}) collective-permute-start(bf16[192,768]{1,0:T(8,128)(2,1)S(1)} %get-tuple-element.37), channel_id=1, source_target_pairs={{0,64},{32,96},{64,0},{96,32},{1,65},{33,97},{65,1},{97,33},{2,66}... | collective-permute-start | bytes 884744 | tf_op jit(solution)/shard_map/ppermute | solution.py:129
  253.7 3.2 %collective-permute-start.9 = (bf16[192,768]{1,0:T(8,128)(2,1)S(1)}, bf16[192,768]{1,0:T(8,128)(2,1)}, u32[]{:S(2)}, u32[]{:S(2)}) collective-permute-start(bf16[192,768]{1,0:T(8,128)(2,1)S(1)} %get-tuple-element.38), channel_id=1, source_target_pairs={{0,96},{32,0},{64,32},{96,64},{1,97},{33,1},{65,33},{97,65},{2,98}... | collective-permute-start | bytes 884744 | tf_op jit(solution)/shard_map/ppermute | solution.py:129
  256.9 1.4 convert_add_fusion
  258.3 6.2 %collective-permute-start.6 = (bf16[128,768]{1,0:T(8,128)(2,1)S(1)}, bf16[128,768]{1,0:T(8,128)(2,1)S(1)}, u32[]{:S(2)}, u32[]{:S(2)}) collective-permute-start(bf16[128,768]{1,0:T(8,128)(2,1)S(1)} %fusion.12), channel_id=1, source_target_pairs={{0,512},{512,0},{1,513},{513,1},{2,514},{514,2},{3,515},{515,3},{4... | collective-permute-start | bytes 589832 | tf_op jit(solution)/shard_map/ppermute | solution.py:129
  264.6 10.2 %all-to-all-done.1 = f32[128,1,6]{2,1,0:T(1,128)S(1)} async-done(((f32[128,1,6]{2,1,0:T(1,128)}), f32[128,1,6]{2,1,0:T(1,128)S(1)}, u32[]{:S(2)}, u32[]{:S(2)}) %all-to-all-start.1) | async-done | bytes 3104 | tf_op jit(solution)/shard_map/all_to_all | solution.py:168
  274.8 0.5 broadcast.24
  275.3 0.8 reduce.4
  276.4 0.5 bitcast_divide_fusion
  276.9 0.7 fusion.13
  277.6 1.5 fusion.11
  279.1 0.9 pad_maximum_fusion
  (28 shorter events, 0.6 us)
Async XLA Ops:
  0.6 1.2 copy-start.2
  1.9 0.7 copy-start.3
  2.5 0.7 copy-start.5
  6.8 160.2 %all-to-all-start = ((bf16[128,48,128]{2,1,0:T(8,128)(2,1)}), bf16[128,48,128]{2,1,0:T(8,128)(2,1)S(1)}, u32[]{:S(2)}, u32[]{:S(2)}) async-start(bf16[128,48,128]{2,1,0:T(8,128)(2,1)} %bitcast.3), calls=%async_computation | async-start | bytes 3145728 | tf_op jit(solution)/shard_map/all_to_all | solution.py:135
  42.2 0.7 copy-start.4
  42.2 1.1 copy-start.9
  43.4 18.7 %collective-permute-start = (bf16[192,768]{1,0:T(8,128)(2,1)S(1)}, bf16[192,768]{1,0:T(8,128)(2,1)}, u32[]{:S(2)}, u32[]{:S(2)}) collective-permute-start(bf16[192,768]{1,0:T(8,128)(2,1)S(1)} %fusion.1), channel_id=1, source_target_pairs={{0,96},{32,0},{64,32},{96,64},{1,97},{33,1},{65,33},{97,65},{2,98}... | collective-permute-start | bytes 884744 | tf_op jit(solution)/shard_map/ppermute | solution.py:129
  48.2 15.6 %collective-permute-start.1 = (bf16[192,768]{1,0:T(8,128)(2,1)S(1)}, bf16[192,768]{1,0:T(8,128)(2,1)}, u32[]{:S(2)}, u32[]{:S(2)}) collective-permute-start(bf16[192,768]{1,0:T(8,128)(2,1)S(1)} %fusion.1), channel_id=1, source_target_pairs={{0,64},{32,96},{64,0},{96,32},{1,65},{33,97},{65,1},{97,33},{2,66}... | collective-permute-start | bytes 884744 | tf_op jit(solution)/shard_map/ppermute | solution.py:129
  50.6 17.2 %collective-permute-start.2 = (bf16[192,768]{1,0:T(8,128)(2,1)S(1)}, bf16[192,768]{1,0:T(8,128)(2,1)}, u32[]{:S(2)}, u32[]{:S(2)}) collective-permute-start(bf16[192,768]{1,0:T(8,128)(2,1)S(1)} %fusion.1), channel_id=1, source_target_pairs={{0,32},{32,64},{64,96},{96,0},{1,33},{33,65},{65,97},{97,1},{2,34}... | collective-permute-start | bytes 884744 | tf_op jit(solution)/shard_map/ppermute | solution.py:129
  166.9 1.3 copy-start
  173.3 1.2 copy-start.7
  174.4 64.1 %collective-permute-start.3 = (bf16[256,768]{1,0:T(8,128)(2,1)}, bf16[256,768]{1,0:T(8,128)(2,1)}, u32[]{:S(2)}, u32[]{:S(2)}) collective-permute-start(bf16[256,768]{1,0:T(8,128)(2,1)} %get-tuple-element.24), channel_id=1, source_target_pairs={{0,128},{128,256},{256,384},{384,0},{1,129},{129,257},{257,385},{3... | collective-permute-start | bytes 1179656 | tf_op jit(solution)/shard_map/ppermute | solution.py:129
  209.6 47.2 %collective-permute-start.4 = (bf16[256,768]{1,0:T(8,128)(2,1)}, bf16[256,768]{1,0:T(8,128)(2,1)}, u32[]{:S(2)}, u32[]{:S(2)}) collective-permute-start(bf16[256,768]{1,0:T(8,128)(2,1)} %get-tuple-element.33), channel_id=1, source_target_pairs={{0,256},{128,384},{256,0},{384,128},{1,257},{129,385},{257,1},{385... | collective-permute-start | bytes 1179656 | tf_op jit(solution)/shard_map/ppermute | solution.py:129
  212.7 44.2 %collective-permute-start.5 = (bf16[256,768]{1,0:T(8,128)(2,1)}, bf16[256,768]{1,0:T(8,128)(2,1)}, u32[]{:S(2)}, u32[]{:S(2)}) collective-permute-start(bf16[256,768]{1,0:T(8,128)(2,1)} %get-tuple-element.34), channel_id=1, source_target_pairs={{0,384},{128,0},{256,128},{384,256},{1,385},{129,1},{257,129},{385... | collective-permute-start | bytes 1179656 | tf_op jit(solution)/shard_map/ppermute | solution.py:129
  215.0 1.3 copy-start.1
  216.2 1.4 copy-start.8
  219.4 57.0 %copy-start.6 = (bf16[128,1]{0,1:T(2,128)(2,1)S(1)}, bf16[128,1]{0,1:T(2,128)(2,1)}, u32[]{:S(2)}) copy-start(bf16[128,1]{0,1:T(2,128)(2,1)} %param.7) | copy-start | bytes 772
  219.4 58.3 %copy-start.10 = (bf16[1,1,192,1536]{3,2,1,0:T(8,128)(2,1)S(1)}, bf16[1,1,192,1536]{3,2,1,0:T(8,128)(2,1)}, u32[]{:S(2)}) copy-start(bf16[1,1,192,1536]{3,2,1,0:T(8,128)(2,1)} %param.9) | copy-start | bytes 1769476
  239.4 35.4 %all-to-all-start.1 = ((f32[128,1,6]{2,1,0:T(1,128)}), f32[128,1,6]{2,1,0:T(1,128)S(1)}, u32[]{:S(2)}, u32[]{:S(2)}) async-start(f32[128,1,6]{2,1,0:T(1,128)} %bitcast.18), calls=%async_computation.1 | async-start | bytes 131072 | tf_op jit(solution)/shard_map/all_to_all | solution.py:168
  245.5 32.1 %collective-permute-start.7 = (bf16[192,768]{1,0:T(8,128)(2,1)S(1)}, bf16[192,768]{1,0:T(8,128)(2,1)S(1)}, u32[]{:S(2)}, u32[]{:S(2)}) collective-permute-start(bf16[192,768]{1,0:T(8,128)(2,1)S(1)} %get-tuple-element.36), channel_id=1, source_target_pairs={{0,32},{32,64},{64,96},{96,0},{1,33},{33,65},{65,97},{97,1},{2,34}... | collective-permute-start | bytes 884744 | tf_op jit(solution)/shard_map/ppermute | solution.py:129
  248.7 29.0 %collective-permute-start.8 = (bf16[192,768]{1,0:T(8,128)(2,1)S(1)}, bf16[192,768]{1,0:T(8,128)(2,1)}, u32[]{:S(2)}, u32[]{:S(2)}) collective-permute-start(bf16[192,768]{1,0:T(8,128)(2,1)S(1)} %get-tuple-element.37), channel_id=1, source_target_pairs={{0,64},{32,96},{64,0},{96,32},{1,65},{33,97},{65,1},{97,33},{2,66}... | collective-permute-start | bytes 884744 | tf_op jit(solution)/shard_map/ppermute | solution.py:129
  253.7 23.9 %collective-permute-start.9 = (bf16[192,768]{1,0:T(8,128)(2,1)S(1)}, bf16[192,768]{1,0:T(8,128)(2,1)}, u32[]{:S(2)}, u32[]{:S(2)}) collective-permute-start(bf16[192,768]{1,0:T(8,128)(2,1)S(1)} %get-tuple-element.38), channel_id=1, source_target_pairs={{0,96},{32,0},{64,32},{96,64},{1,97},{33,1},{65,33},{97,65},{2,98}... | collective-permute-start | bytes 884744 | tf_op jit(solution)/shard_map/ppermute | solution.py:129
  258.3 18.6 %collective-permute-start.6 = (bf16[128,768]{1,0:T(8,128)(2,1)S(1)}, bf16[128,768]{1,0:T(8,128)(2,1)S(1)}, u32[]{:S(2)}, u32[]{:S(2)}) collective-permute-start(bf16[128,768]{1,0:T(8,128)(2,1)S(1)} %fusion.12), channel_id=1, source_target_pairs={{0,512},{512,0},{1,513},{513,1},{2,514},{514,2},{3,515},{515,3},{4... | collective-permute-start | bytes 589832 | tf_op jit(solution)/shard_map/ppermute | solution.py:129

commit v4 on v3

v4 whole, which is shorter than its diff:
```python
import jax
import jax.numpy as jnp
from jax import lax
from jax.experimental import pallas as pl
from jax.experimental.pallas import tpu as pltpu
from jax.sharding import Mesh
from jax.sharding import PartitionSpec as P

BF16, F32, I32 = jnp.bfloat16, jnp.float32, jnp.int32
ZA, ZB, X, ZH, Y, C = 2, 4, 4, 4, 4, 2
ZL = ZA * ZB
E = ZH * Y * C
CAP = 6
TOK = 128
FFW = 768
LANES = 128
EXPERT = ("zh", "y", "c")
BLOCK = ZB * CAP
FAN = X * E
SLOTS = E * CAP
ROWS = X * SLOTS
WIDE = ZB * LANES
SUB = 16
VMEM = 24 * 1024 * 1024


def pack_kernel(ids_ref, gate_ref, grad_ref, low_ref, high_ref, keys, gates, grads):
    ids = ids_ref[...]
    onehot = (lax.broadcasted_iota(I32, (E, TOK), 0) == ids).astype(F32)
    earlier = lax.broadcasted_iota(I32, (TOK, TOK), 0) < lax.broadcasted_iota(I32, (TOK, TOK), 1)
    before = jnp.dot(onehot.astype(BF16), earlier.astype(BF16), preferred_element_type=F32)
    place = jnp.sum(before * onehot, axis=0, keepdims=True).astype(I32)
    base = ids * BLOCK + place
    for z in range(ZB):
        keys[:, z * TOK : (z + 1) * TOK] = base + z * CAP
        gates[:, z * TOK : (z + 1) * TOK] = gate_ref[...].astype(F32)
    for z in range(ZL):
        grads[z * TOK : (z + 1) * TOK, :] = grad_ref[:, z * (X * LANES) : (z + 1) * (X * LANES)]
    step = 8 * BLOCK
    deep = ZB * TOK

    def body(i, carry):
        row = lax.broadcasted_iota(I32, (step, deep), 0) + i * step
        take = jnp.where(row == keys[...], gates[...], 0.0).astype(BF16)
        for h, rows_ref in enumerate((low_ref, high_ref)):
            out = jnp.dot(take, grads[h * deep : (h + 1) * deep, :], preferred_element_type=F32).astype(BF16)
            for q in range(X):
                rows_ref[q, pl.ds(pl.multiple_of(i * step, step), step), :] = out[:, q * LANES : (q + 1) * LANES]
        return carry

    lax.fori_loop(0, E * BLOCK // step, body, 0)


def pack(ids, gates, grad):
    return pl.pallas_call(
        pack_kernel,
        out_shape=[jax.ShapeDtypeStruct((X, E * BLOCK, LANES), BF16)] * ZA,
        scratch_shapes=[
            pltpu.VMEM((1, ZB * TOK), I32),
            pltpu.VMEM((1, ZB * TOK), F32),
            pltpu.VMEM((ZL * TOK, X * LANES), BF16),
        ],
        compiler_params=pltpu.CompilerParams(vmem_limit_bytes=VMEM),
        cost_estimate=pl.CostEstimate(flops=4 * E * BLOCK * ZB * TOK * X * LANES, bytes_accessed=3 << 20, transcendentals=0),
        name="pack",
    )(ids, gates, grad)


def weight_kernel(own_ref, recv_ref, acts_ref, *outs):
    parts, scaled_ref, product = outs[:ZB], outs[ZB], outs[ZB + 1]
    size = SUB * BLOCK
    group = SUB * CAP
    out = lax.broadcasted_iota(I32, (size, size), 0)
    col = lax.broadcasted_iota(I32, (size, size), 1)
    inner = out % group
    source = (inner // CAP) * BLOCK + (out // group) * CAP + inner % CAP
    order = jnp.where(source == col, 1.0, 0.0).astype(BF16)
    for k in range(FAN // SUB):
        rows = jnp.dot(order, recv_ref[k], preferred_element_type=F32).astype(BF16)
        for z in range(ZB):
            scaled_ref[k * group : (k + 1) * group, z * LANES : (z + 1) * LANES] = rows[z * group : (z + 1) * group, :]
    product[...] = lax.dot_general(
        scaled_ref[...], acts_ref[...], (((0,), (0,)), ((), ())), preferred_element_type=F32
    )
    for d in range(ZB):
        at = pl.multiple_of(lax.rem(own_ref[0] + d, ZB) * LANES, LANES)
        parts[d][...] = product[pl.ds(at, LANES), :].astype(BF16)


def weight_part(own, recv, acts):
    vmem = pl.BlockSpec(memory_space=pltpu.VMEM)
    return pl.pallas_call(
        weight_kernel,
        in_specs=[pl.BlockSpec(memory_space=pltpu.SMEM), vmem, vmem],
        out_shape=[jax.ShapeDtypeStruct((LANES, FFW), BF16)] * ZB + [jax.ShapeDtypeStruct((ROWS, WIDE), BF16)],
        scratch_shapes=[pltpu.VMEM((WIDE, FFW), F32)],
        compiler_params=pltpu.CompilerParams(vmem_limit_bytes=VMEM),
        cost_estimate=pl.CostEstimate(flops=4 * ROWS * ROWS * WIDE, bytes_accessed=3 << 20, transcendentals=0),
        name="weight_part",
    )(own, recv.reshape(FAN // SUB, SUB * BLOCK, LANES), acts)


def act_kernel(own_ref, low_ref, high_ref, weight_ref, acts_ref, *outs):
    parts, score_ref, grad = outs[:X], outs[X], outs[X + 1]
    grad[...] = jnp.dot(low_ref[...], weight_ref[0], preferred_element_type=F32)
    grad[...] += jnp.dot(high_ref[...], weight_ref[1], preferred_element_type=F32)
    for d in range(X):
        at = pl.multiple_of(lax.rem(own_ref[0] + d, X) * SLOTS, SLOTS)
        parts[d][...] = grad[pl.ds(at, SLOTS), :].astype(BF16)
    narrow = jnp.zeros((ROWS, LANES), F32)
    for f in range(0, FFW, LANES):
        narrow = narrow + grad[:, f : f + LANES] * acts_ref[:, f : f + LANES].astype(F32)
    score_ref[...] = jnp.sum(narrow.T, axis=0, keepdims=True)


def act_part(own, low, high, weight, acts):
    vmem = pl.BlockSpec(memory_space=pltpu.VMEM)
    return pl.pallas_call(
        act_kernel,
        in_specs=[pl.BlockSpec(memory_space=pltpu.SMEM), vmem, vmem, vmem, vmem],
        out_shape=[jax.ShapeDtypeStruct((SLOTS, FFW), BF16)] * X + [jax.ShapeDtypeStruct((1, ROWS), F32)],
        scratch_shapes=[pltpu.VMEM((ROWS, FFW), F32)],
        compiler_params=pltpu.CompilerParams(vmem_limit_bytes=VMEM),
        cost_estimate=pl.CostEstimate(flops=4 * ROWS * FFW * WIDE, bytes_accessed=6 << 20, transcendentals=0),
        name="act_part",
    )(own, low, high, weight, acts)


def shift(block, axis, n, d):
    return lax.ppermute(block, axis, [(i, (i + d) % n) for i in range(n)])


def exchange(blocks):
    return lax.all_to_all(blocks, ("x",) + EXPERT, split_axis=0, concat_axis=0, tiled=True)


def per_device(out_grad, expert_ids, gate_values, down_weight, gate_up):
    own_x, own_za, own_zb = (lax.axis_index(a) for a in ("x", "za", "zb"))
    rows = pack(expert_ids.reshape(1, TOK), gate_values.reshape(1, TOK), out_grad)
    low = exchange(rows[0].reshape(FAN, BLOCK, LANES))

    saved = gate_up[0, 0]
    gate_act = saved[:, :FFW].astype(F32)
    up_act = saved[:, FFW:].astype(F32)
    sigmoid_val = jax.nn.sigmoid(gate_act)
    silu_val = gate_act * sigmoid_val
    hidden = (silu_val * up_act).astype(BF16)
    weight = lax.dynamic_index_in_dim(down_weight.reshape(ZL, X, LANES, FFW), own_x, 1, keepdims=False)
    weight = weight.reshape(ZA, WIDE, FFW)
    chosen = expert_ids.reshape(TOK)
    onehot = (chosen[:, None] == jnp.arange(E, dtype=I32)[None, :]).astype(F32)
    later = jnp.arange(TOK)[:, None] > jnp.arange(TOK)[None, :]
    before = jnp.dot(later.astype(BF16), onehot.astype(BF16), preferred_element_type=F32)
    slots = chosen * CAP + jnp.sum(before * onehot, axis=1).astype(I32)
    hidden, weight, slots = lax.optimization_barrier((hidden, weight, slots))
    came = [hidden] + [shift(hidden, "x", X, d) for d in range(1, X)]
    turned = [came[-k % X] for k in range(X)]
    acts = lax.dynamic_slice_in_dim(jnp.concatenate(turned + turned), (X - own_x) % X * SLOTS, ROWS, 0)

    low, behind, acts = lax.optimization_barrier((low, rows[1], acts))
    high = exchange(behind.reshape(FAN, BLOCK, LANES))
    own_zb = own_zb.reshape(1)
    *sums, scaled_low = weight_part(own_zb, low, acts)
    first = [sums[0]] + [shift(sums[d], "zb", ZB, d) for d in range(1, ZB)]
    high, first = lax.optimization_barrier((high, first))
    *sums, scaled_high = weight_part(own_zb, high, acts)
    second = [sums[0]] + [shift(sums[d], "zb", ZB, d) for d in range(1, ZB)]
    *parts, score = act_part(own_x.reshape(1), scaled_low, scaled_high, weight, acts)
    second[1], parts, score = lax.optimization_barrier((second[1], parts, score))
    near = jnp.stack([sum(part.astype(F32) for part in half) for half in (first, second)])
    away = lax.dynamic_index_in_dim(near, 1 - own_za, 0, keepdims=False).astype(BF16)
    stay = lax.dynamic_index_in_dim(near, own_za, 0, keepdims=False)
    weight_share = (stay + shift(away, "za", ZA, 1).astype(F32)).astype(BF16)

    returned = exchange(score.reshape(FAN, 1, CAP))
    hidden_grad = parts[0].astype(F32)
    for d in range(1, X):
        hidden_grad = hidden_grad + shift(parts[d], "x", X, d).astype(F32)
    gate_part = hidden_grad * up_act * sigmoid_val * (1.0 + gate_act * (1.0 - sigmoid_val))
    up_part = hidden_grad * silu_val
    gu_grad = jnp.concatenate([gate_part, up_part], axis=1).astype(BF16)

    returned = jnp.sum(returned.reshape(X, SLOTS), axis=0)
    hit = slots[:, None] == jnp.arange(SLOTS, dtype=I32)[None, :]
    route = jnp.sum(jnp.where(hit, returned[None, :], 0.0), axis=1)
    route_grad = route.reshape(TOK, 1) / gate_values.astype(F32)
    return (weight_share[None], gu_grad[None, None], route_grad)


def solution(mesh):
    fine = Mesh(mesh.devices.reshape(ZA, ZB, X, ZH, Y, C), ("za", "zb", "x", "zh", "y", "c"))
    dp = ("za", "zb", "x")
    return jax.shard_map(
        per_device,
        mesh=fine,
        in_specs=(
            P(dp + EXPERT, None),
            P(dp + EXPERT, None),
            P(dp + EXPERT, None),
            P(EXPERT, None, None),
            P(dp, EXPERT, None, None),
        ),
        out_specs=(
            P(EXPERT, dp, None),
            P(dp, EXPERT, None, None),
            P(dp + EXPERT, None),
        ),
        check_vma=False,
    )
```

time: 281 us -> 310 us (1.10)
  the two profiles are of different devices: /device:TPU:64 before, /device:TPU:24 now
where the time goes in v4:
time: 310 us; the launch traced here: 308 us
  waiting for transfers between devices  147 us (47%)
  starting transfers between devices  128 us (41%)
  local copies, waits for them, and re-layouts  14.3 us (5%)
  Pallas kernels  11.7 us (4%)
  other arithmetic  5.09 us (2%)
    ppermute x13, waiting for transfers between devices, shift(): return lax.ppermute(block, axis, [(i, (i + d) % n) for i in range(n)])  82.7 us
    all_to_all x3, starting transfers between devices, exchange(): lax.all_to_all(blocks, ('x',) + EXPERT, split_axis=0, concat_axis=0, tile...  75.5 us
    all_to_all x3, waiting for transfers between devices, exchange(): lax.all_to_all(blocks, ('x',) + EXPERT, split_axis=0, concat_axis=0, tile...  64.5 us
    ppermute x13, starting transfers between devices, shift(): return lax.ppermute(block, axis, [(i, (i + d) % n) for i in range(n)])  52.7 us
    unnamed x43, local copies, waits for them, and re-layouts  9.36 us
    pallas_call x2, Pallas kernels, weight_part(): pl.pallas_call(weight_kernel, in_specs=[pl.BlockSpec(memory_space=pltpu.S...  6.54 us
  transfers between devices with their start and end apart: 16, of which 8 were waited for; matrix products, arithmetic and copies ran while one was open for 5% of the time, Pallas kernels for 2%

profile of v4, /device:TPU:24, one launch (start us, length us, event | category | flops | bytes accessed | tf_op | source)
XLA Modules:
  0.0 307.7 jit_solution(17161515045649864139)
XLA Ops:
  0.6 1.2 copy-done.2
  1.9 0.7 copy-done.3
  2.5 0.7 copy-done.5
  3.2 2.7 pack.1
  5.9 35.1 %all-to-all-start = ((bf16[128,24,128]{2,1,0:T(8,128)(2,1)}), bf16[128,24,128]{2,1,0:T(8,128)(2,1)S(1)}, u32[]{:S(2)}, u32[]{:S(2)}) async-start(bf16[128,24,128]{2,1,0:T(8,128)(2,1)} %bitcast.2), calls=%async_computation | async-start | bytes 1572864 | tf_op jit(solution)/shard_map/all_to_all | solution.py:134
  41.2 1.5 constant_dynamic-slice_fusion.1
  42.9 5.2 %collective-permute-start = (bf16[192,768]{1,0:T(8,128)(2,1)S(1)}, bf16[192,768]{1,0:T(8,128)(2,1)S(1)}, u32[]{:S(2)}, u32[]{:S(2)}) collective-permute-start(bf16[192,768]{1,0:T(8,128)(2,1)S(1)} %fusion.1), channel_id=1, source_target_pairs={{0,96},{32,0},{64,32},{96,64},{1,97},{33,1},{65,33},{97,65},{2,98}... | collective-permute-start | bytes 884744 | tf_op jit(solution)/shard_map/ppermute | solution.py:130
  48.1 2.3 collective-permute-start.1
  50.4 3.0 collective-permute-start.2
  53.4 0.7 constant_dynamic-update-slice_fusion.7
  54.2 9.2 %collective-permute-done = bf16[192,768]{1,0:T(8,128)(2,1)S(1)} collective-permute-done((bf16[192,768]{1,0:T(8,128)(2,1)S(1)}, bf16[192,768]{1,0:T(8,128)(2,1)S(1)}, u32[]{:S(2)}, u32[]{:S(2)}) %collective-permute-start) | collective-permute-done | bytes 294944 | tf_op jit(solution)/shard_map/ppermute | solution.py:130
  63.4 0.7 constant_dynamic-update-slice_fusion.6
  64.1 0.8 constant_dynamic-update-slice_fusion.5
  64.9 5.5 %collective-permute-done.2 = bf16[192,768]{1,0:T(8,128)(2,1)S(1)} collective-permute-done((bf16[192,768]{1,0:T(8,128)(2,1)S(1)}, bf16[192,768]{1,0:T(8,128)(2,1)S(1)}, u32[]{:S(2)}, u32[]{:S(2)}) %collective-permute-start.2) | collective-permute-done | bytes 294944 | tf_op jit(solution)/shard_map/ppermute | solution.py:130
  70.3 0.8 constant_dynamic-update-slice_fusion.4
  71.1 0.7 constant_dynamic-update-slice_fusion.3
  71.8 0.7 constant_dynamic-update-slice_fusion.2
  72.6 0.7 constant_dynamic-update-slice_fusion.1
  73.3 0.7 constant_dynamic-update-slice_fusion
  74.0 1.3 constant_dynamic-slice_fusion.acts_ref
  75.4 43.4 %all-to-all-done = bf16[128,24,128]{2,1,0:T(8,128)(2,1)S(1)} async-done(((bf16[128,24,128]{2,1,0:T(8,128)(2,1)}), bf16[128,24,128]{2,1,0:T(8,128)(2,1)S(1)}, u32[]{:S(2)}, u32[]{:S(2)}) %all-to-all-start) | async-done | bytes 786464 | tf_op jit(solution)/shard_map/all_to_all | solution.py:134
  118.7 19.9 %all-to-all-start.1 = ((bf16[128,24,128]{2,1,0:T(8,128)(2,1)}), bf16[128,24,128]{2,1,0:T(8,128)(2,1)}, u32[]{:S(2)}, u32[]{:S(2)}) async-start(bf16[128,24,128]{2,1,0:T(8,128)(2,1)} %bitcast.7), calls=%async_computation.1 | async-start | bytes 1572864 | tf_op jit(solution)/shard_map/all_to_all | solution.py:134
  138.7 2.7 weight_part.2
  141.3 0.7 copy-done
  142.0 0.9 copy-done.7
  142.9 3.6 %collective-permute-start.3 = (bf16[128,768]{1,0:T(8,128)(2,1)}, bf16[128,768]{1,0:T(8,128)(2,1)S(1)}, u32[]{:S(2)}, u32[]{:S(2)}) collective-permute-start(bf16[128,768]{1,0:T(8,128)(2,1)} %get-tuple-element.44), channel_id=1, source_target_pairs={{0,128},{128,256},{256,384},{384,0},{1,129},{129,257},{257,385},{3... | collective-permute-start | bytes 589832 | tf_op jit(solution)/shard_map/ppermute | solution.py:130
  146.5 3.2 %collective-permute-start.4 = (bf16[128,768]{1,0:T(8,128)(2,1)}, bf16[128,768]{1,0:T(8,128)(2,1)S(1)}, u32[]{:S(2)}, u32[]{:S(2)}) collective-permute-start(bf16[128,768]{1,0:T(8,128)(2,1)} %get-tuple-element.45), channel_id=1, source_target_pairs={{0,256},{128,384},{256,0},{384,128},{1,257},{129,385},{257,1},{385... | collective-permute-start | bytes 589832 | tf_op jit(solution)/shard_map/ppermute | solution.py:130
  149.7 3.0 collective-permute-start.5
  152.7 50.4 %collective-permute-done.3 = bf16[128,768]{1,0:T(8,128)(2,1)S(1)} collective-permute-done((bf16[128,768]{1,0:T(8,128)(2,1)}, bf16[128,768]{1,0:T(8,128)(2,1)S(1)}, u32[]{:S(2)}, u32[]{:S(2)}) %collective-permute-start.3) | collective-permute-done | bytes 196640 | tf_op jit(solution)/shard_map/ppermute | solution.py:130
  203.1 13.6 %collective-permute-done.4 = bf16[128,768]{1,0:T(8,128)(2,1)S(1)} collective-permute-done((bf16[128,768]{1,0:T(8,128)(2,1)}, bf16[128,768]{1,0:T(8,128)(2,1)S(1)}, u32[]{:S(2)}, u32[]{:S(2)}) %collective-permute-start.4) | collective-permute-done | bytes 196640 | tf_op jit(solution)/shard_map/ppermute | solution.py:130
  216.8 1.7 collective-permute-done.5
  218.5 3.9 %weight_part.3 = (bf16[128,768]{1,0:T(8,128)(2,1)S(1)}, bf16[128,768]{1,0:T(8,128)(2,1)S(1)}, bf16[128,768]{1,0:T(8,128)(2,1)}, bf16[128,768]{1,0:T(8,128)(2,1)}, bf16[768,512]{1,0:T(8,128)(2,1)S(1)}) custom-call(s32[1]{0:T(128)} %bitcast.8.own_ref, bf16[8,384,128]{2,1,0:T(8,128)(2,1)} %bitcast.11.recv_ref, ...), custom_call_target="tpu_custom_call" | custom-call | flops 1207959552 | bytes 3145728 | tf_op jit(solution)/shard_map/weight_part/pallas_call | solution.py:92
  222.4 13.6 %collective-permute-start.6 = (bf16[128,768]{1,0:T(8,128)(2,1)S(1)}, bf16[128,768]{1,0:T(8,128)(2,1)S(1)}, u32[]{:S(2)}, u32[]{:S(2)}) collective-permute-start(bf16[128,768]{1,0:T(8,128)(2,1)S(1)} %get-tuple-element.53), channel_id=1, source_target_pairs={{0,128},{128,256},{256,384},{384,0},{1,129},{129,257},{257,385},{3... | collective-permute-start | bytes 589832 | tf_op jit(solution)/shard_map/ppermute | solution.py:130
  235.9 1.9 collective-permute-start.7
  237.9 4.3 %collective-permute-start.8 = (bf16[128,768]{1,0:T(8,128)(2,1)}, bf16[128,768]{1,0:T(8,128)(2,1)}, u32[]{:S(2)}, u32[]{:S(2)}) collective-permute-start(bf16[128,768]{1,0:T(8,128)(2,1)} %get-tuple-element.64), channel_id=1, source_target_pairs={{0,384},{128,0},{256,128},{384,256},{1,385},{129,1},{257,129},{385... | collective-permute-start | bytes 589832 | tf_op jit(solution)/shard_map/ppermute | solution.py:130
  242.2 2.5 act_part.1
  244.9 2.5 collective-permute-start.10
  247.4 3.7 %collective-permute-start.11 = (bf16[192,768]{1,0:T(8,128)(2,1)}, bf16[192,768]{1,0:T(8,128)(2,1)S(1)}, u32[]{:S(2)}, u32[]{:S(2)}) collective-permute-start(bf16[192,768]{1,0:T(8,128)(2,1)} %get-tuple-element.67), channel_id=1, source_target_pairs={{0,64},{32,96},{64,0},{96,32},{1,65},{33,97},{65,1},{97,33},{2,66}... | collective-permute-start | bytes 884744 | tf_op jit(solution)/shard_map/ppermute | solution.py:130
  251.1 4.0 %collective-permute-start.12 = (bf16[192,768]{1,0:T(8,128)(2,1)S(1)}, bf16[192,768]{1,0:T(8,128)(2,1)S(1)}, u32[]{:S(2)}, u32[]{:S(2)}) collective-permute-start(bf16[192,768]{1,0:T(8,128)(2,1)S(1)} %get-tuple-element.68), channel_id=1, source_target_pairs={{0,96},{32,0},{64,32},{96,64},{1,97},{33,1},{65,33},{97,65},{2,98}... | collective-permute-start | bytes 884744 | tf_op jit(solution)/shard_map/ppermute | solution.py:130
  255.2 0.8 reshape.94
  255.9 20.4 %all-to-all-start.2 = ((f32[128,1,6]{2,1,0:T(1,128)}), f32[128,1,6]{2,1,0:T(1,128)S(1)}, u32[]{:S(2)}, u32[]{:S(2)}) async-start(f32[128,1,6]{2,1,0:T(1,128)} %bitcast.19), calls=%async_computation.2 | async-start | bytes 131072 | tf_op jit(solution)/shard_map/all_to_all | solution.py:134
  276.4 1.2 add_bitcast_fusion
  277.7 2.6 collective-permute-start.9
  280.2 21.1 %all-to-all-done.2 = f32[128,1,6]{2,1,0:T(1,128)S(1)} async-done(((f32[128,1,6]{2,1,0:T(1,128)}), f32[128,1,6]{2,1,0:T(1,128)S(1)}, u32[]{:S(2)}, u32[]{:S(2)}) %all-to-all-start.2) | async-done | bytes 3104 | tf_op jit(solution)/shard_map/all_to_all | solution.py:134
  301.9 0.8 reduce.4
  303.5 2.2 collective-permute-done.9
  305.7 0.8 fusion.17
  306.9 0.9 pad_maximum_fusion
  (51 shorter events, 2.3 us)
Async XLA Ops:
  0.6 40.4 %copy-start.4 = (s32[128,1]{0,1:T(1,128)S(1)}, s32[128,1]{0,1:T(1,128)}, u32[]{:S(2)}) copy-start(s32[128,1]{0,1:T(1,128)} %param.6) | copy-start | bytes 1540
  0.6 1.2 copy-start.2
  1.9 0.7 copy-start.3
  2.5 0.7 copy-start.5
  5.9 36.9 %copy-start.9 = (bf16[1,1,192,1536]{3,2,1,0:T(8,128)(2,1)S(1)}, bf16[1,1,192,1536]{3,2,1,0:T(8,128)(2,1)}, u32[]{:S(2)}) copy-start(bf16[1,1,192,1536]{3,2,1,0:T(8,128)(2,1)} %param.9) | copy-start | bytes 1769476
  5.9 112.8 %all-to-all-start = ((bf16[128,24,128]{2,1,0:T(8,128)(2,1)}), bf16[128,24,128]{2,1,0:T(8,128)(2,1)S(1)}, u32[]{:S(2)}, u32[]{:S(2)}) async-start(bf16[128,24,128]{2,1,0:T(8,128)(2,1)} %bitcast.2), calls=%async_computation | async-start | bytes 1572864 | tf_op jit(solution)/shard_map/all_to_all | solution.py:134
  42.9 20.4 %collective-permute-start = (bf16[192,768]{1,0:T(8,128)(2,1)S(1)}, bf16[192,768]{1,0:T(8,128)(2,1)S(1)}, u32[]{:S(2)}, u32[]{:S(2)}) collective-permute-start(bf16[192,768]{1,0:T(8,128)(2,1)S(1)} %fusion.1), channel_id=1, source_target_pairs={{0,96},{32,0},{64,32},{96,64},{1,97},{33,1},{65,33},{97,65},{2,98}... | collective-permute-start | bytes 884744 | tf_op jit(solution)/shard_map/ppermute | solution.py:130
  48.1 16.0 %collective-permute-start.1 = (bf16[192,768]{1,0:T(8,128)(2,1)S(1)}, bf16[192,768]{1,0:T(8,128)(2,1)S(1)}, u32[]{:S(2)}, u32[]{:S(2)}) collective-permute-start(bf16[192,768]{1,0:T(8,128)(2,1)S(1)} %fusion.1), channel_id=1, source_target_pairs={{0,64},{32,96},{64,0},{96,32},{1,65},{33,97},{65,1},{97,33},{2,66}... | collective-permute-start | bytes 884744 | tf_op jit(solution)/shard_map/ppermute | solution.py:130
  50.4 19.9 %collective-permute-start.2 = (bf16[192,768]{1,0:T(8,128)(2,1)S(1)}, bf16[192,768]{1,0:T(8,128)(2,1)S(1)}, u32[]{:S(2)}, u32[]{:S(2)}) collective-permute-start(bf16[192,768]{1,0:T(8,128)(2,1)S(1)} %fusion.1), channel_id=1, source_target_pairs={{0,32},{32,64},{64,96},{96,0},{1,33},{33,65},{65,97},{97,1},{2,34}... | collective-permute-start | bytes 884744 | tf_op jit(solution)/shard_map/ppermute | solution.py:130
  118.7 99.8 %all-to-all-start.1 = ((bf16[128,24,128]{2,1,0:T(8,128)(2,1)}), bf16[128,24,128]{2,1,0:T(8,128)(2,1)}, u32[]{:S(2)}, u32[]{:S(2)}) async-start(bf16[128,24,128]{2,1,0:T(8,128)(2,1)} %bitcast.7), calls=%async_computation.1 | async-start | bytes 1572864 | tf_op jit(solution)/shard_map/all_to_all | solution.py:134
  141.3 0.7 copy-start
  142.0 0.9 copy-start.7
  142.9 60.2 %collective-permute-start.3 = (bf16[128,768]{1,0:T(8,128)(2,1)}, bf16[128,768]{1,0:T(8,128)(2,1)S(1)}, u32[]{:S(2)}, u32[]{:S(2)}) collective-permute-start(bf16[128,768]{1,0:T(8,128)(2,1)} %get-tuple-element.44), channel_id=1, source_target_pairs={{0,128},{128,256},{256,384},{384,0},{1,129},{129,257},{257,385},{3... | collective-permute-start | bytes 589832 | tf_op jit(solution)/shard_map/ppermute | solution.py:130
  146.5 70.3 %collective-permute-start.4 = (bf16[128,768]{1,0:T(8,128)(2,1)}, bf16[128,768]{1,0:T(8,128)(2,1)S(1)}, u32[]{:S(2)}, u32[]{:S(2)}) collective-permute-start(bf16[128,768]{1,0:T(8,128)(2,1)} %get-tuple-element.45), channel_id=1, source_target_pairs={{0,256},{128,384},{256,0},{384,128},{1,257},{129,385},{257,1},{385... | collective-permute-start | bytes 589832 | tf_op jit(solution)/shard_map/ppermute | solution.py:130
  149.7 68.8 %collective-permute-start.5 = (bf16[128,768]{1,0:T(8,128)(2,1)}, bf16[128,768]{1,0:T(8,128)(2,1)S(1)}, u32[]{:S(2)}, u32[]{:S(2)}) collective-permute-start(bf16[128,768]{1,0:T(8,128)(2,1)} %get-tuple-element.46), channel_id=1, source_target_pairs={{0,384},{128,0},{256,128},{384,256},{1,385},{129,1},{257,129},{385... | collective-permute-start | bytes 589832 | tf_op jit(solution)/shard_map/ppermute | solution.py:130
  203.1 39.0 %copy-start.11 = (bf16[128,768]{1,0:T(8,128)(2,1)}, bf16[128,768]{1,0:T(8,128)(2,1)S(1)}, u32[]{:S(2)}) copy-start(bf16[128,768]{1,0:T(8,128)(2,1)S(1)} %collective-permute-done.3) | copy-start | bytes 589828
  216.8 25.4 %copy-start.13 = (bf16[128,768]{1,0:T(8,128)(2,1)}, bf16[128,768]{1,0:T(8,128)(2,1)S(1)}, u32[]{:S(2)}) copy-start(bf16[128,768]{1,0:T(8,128)(2,1)S(1)} %collective-permute-done.4) | copy-start | bytes 589828
  218.5 23.7 %copy-start.15 = (bf16[128,768]{1,0:T(8,128)(2,1)}, bf16[128,768]{1,0:T(8,128)(2,1)S(1)}, u32[]{:S(2)}) copy-start(bf16[128,768]{1,0:T(8,128)(2,1)S(1)} %collective-permute-done.5) | copy-start | bytes 589828
  218.5 23.7 %copy-start.8 = (bf16[768,512]{1,0:T(8,128)(2,1)S(1)}, bf16[768,512]{1,0:T(8,128)(2,1)}, u32[]{:S(2)}) copy-start(bf16[768,512]{1,0:T(8,128)(2,1)} %copy-done.7) | copy-start | bytes 2359300
  222.4 22.4 %copy-start.1 = (bf16[128,768]{1,0:T(8,128)(2,1)S(1)}, bf16[128,768]{1,0:T(8,128)(2,1)}, u32[]{:S(2)}) copy-start(bf16[128,768]{1,0:T(8,128)(2,1)} %copy-done) | copy-start | bytes 589828
  222.4 22.5 %collective-permute-start.6 = (bf16[128,768]{1,0:T(8,128)(2,1)S(1)}, bf16[128,768]{1,0:T(8,128)(2,1)S(1)}, u32[]{:S(2)}, u32[]{:S(2)}) collective-permute-start(bf16[128,768]{1,0:T(8,128)(2,1)S(1)} %get-tuple-element.53), channel_id=1, source_target_pairs={{0,128},{128,256},{256,384},{384,0},{1,129},{129,257},{257,385},{3... | collective-permute-start | bytes 589832 | tf_op jit(solution)/shard_map/ppermute | solution.py:130
  235.9 40.4 %collective-permute-start.7 = (bf16[128,768]{1,0:T(8,128)(2,1)}, bf16[128,768]{1,0:T(8,128)(2,1)}, u32[]{:S(2)}, u32[]{:S(2)}) collective-permute-start(bf16[128,768]{1,0:T(8,128)(2,1)} %get-tuple-element.63), channel_id=1, source_target_pairs={{0,256},{128,384},{256,0},{384,128},{1,257},{129,385},{257,1},{385... | collective-permute-start | bytes 589832 | tf_op jit(solution)/shard_map/ppermute | solution.py:130
  237.9 38.5 %collective-permute-start.8 = (bf16[128,768]{1,0:T(8,128)(2,1)}, bf16[128,768]{1,0:T(8,128)(2,1)}, u32[]{:S(2)}, u32[]{:S(2)}) collective-permute-start(bf16[128,768]{1,0:T(8,128)(2,1)} %get-tuple-element.64), channel_id=1, source_target_pairs={{0,384},{128,0},{256,128},{384,256},{1,385},{129,1},{257,129},{385... | collective-permute-start | bytes 589832 | tf_op jit(solution)/shard_map/ppermute | solution.py:130
  242.2 2.5 copy-start.12
  242.2 2.5 copy-start.14
  242.2 2.5 copy-start.16
  244.7 58.2 %copy-start.6 = (bf16[128,1]{0,1:T(2,128)(2,1)S(1)}, bf16[128,1]{0,1:T(2,128)(2,1)}, u32[]{:S(2)}) copy-start(bf16[128,1]{0,1:T(2,128)(2,1)} %param.7) | copy-start | bytes 772
  244.8 61.7 %copy-start.10 = (bf16[1,1,192,1536]{3,2,1,0:T(8,128)(2,1)S(1)}, bf16[1,1,192,1536]{3,2,1,0:T(8,128)(2,1)}, u32[]{:S(2)}) copy-start(bf16[1,1,192,1536]{3,2,1,0:T(8,128)(2,1)} %param.9) | copy-start | bytes 1769476
  244.9 2.5 copy-start.17
  244.9 61.5 %collective-permute-start.10 = (bf16[192,768]{1,0:T(8,128)(2,1)}, bf16[192,768]{1,0:T(8,128)(2,1)S(1)}, u32[]{:S(2)}, u32[]{:S(2)}) collective-permute-start(bf16[192,768]{1,0:T(8,128)(2,1)} %get-tuple-element.66), channel_id=1, source_target_pairs={{0,32},{32,64},{64,96},{96,0},{1,33},{33,65},{65,97},{97,1},{2,34}... | collective-permute-start | bytes 884744 | tf_op jit(solution)/shard_map/ppermute | solution.py:130
  247.4 59.0 %collective-permute-start.11 = (bf16[192,768]{1,0:T(8,128)(2,1)}, bf16[192,768]{1,0:T(8,128)(2,1)S(1)}, u32[]{:S(2)}, u32[]{:S(2)}) collective-permute-start(bf16[192,768]{1,0:T(8,128)(2,1)} %get-tuple-element.67), channel_id=1, source_target_pairs={{0,64},{32,96},{64,0},{96,32},{1,65},{33,97},{65,1},{97,33},{2,66}... | collective-permute-start | bytes 884744 | tf_op jit(solution)/shard_map/ppermute | solution.py:130
  251.1 55.3 %collective-permute-start.12 = (bf16[192,768]{1,0:T(8,128)(2,1)S(1)}, bf16[192,768]{1,0:T(8,128)(2,1)S(1)}, u32[]{:S(2)}, u32[]{:S(2)}) collective-permute-start(bf16[192,768]{1,0:T(8,128)(2,1)S(1)} %get-tuple-element.68), channel_id=1, source_target_pairs={{0,96},{32,0},{64,32},{96,64},{1,97},{33,1},{65,33},{97,65},{2,98}... | collective-permute-start | bytes 884744 | tf_op jit(solution)/shard_map/ppermute | solution.py:130
  255.9 45.4 %all-to-all-start.2 = ((f32[128,1,6]{2,1,0:T(1,128)}), f32[128,1,6]{2,1,0:T(1,128)S(1)}, u32[]{:S(2)}, u32[]{:S(2)}) async-start(f32[128,1,6]{2,1,0:T(1,128)} %bitcast.19), calls=%async_computation.2 | async-start | bytes 131072 | tf_op jit(solution)/shard_map/all_to_all | solution.py:134
  277.7 28.0 %collective-permute-start.9 = (bf16[128,768]{1,0:T(8,128)(2,1)S(1)}, bf16[128,768]{1,0:T(8,128)(2,1)S(1)}, u32[]{:S(2)}, u32[]{:S(2)}) collective-permute-start(bf16[128,768]{1,0:T(8,128)(2,1)S(1)} %fusion.18), channel_id=1, source_target_pairs={{0,512},{512,0},{1,513},{513,1},{2,514},{514,2},{3,515},{515,3},{4... | collective-permute-start | bytes 589832 | tf_op jit(solution)/shard_map/ppermute | solution.py:130

commit v5 on v3

--- a/solution.py
+++ b/solution.py
@@ -100,29 +100,27 @@
     )(own, recv, acts)
 
 
-def act_kernel(own_ref, scaled_ref, weight_ref, acts_ref, *outs):
-    parts, score_ref, grad = outs[:X], outs[X], outs[X + 1]
+def act_kernel(scaled_ref, weight_ref, acts_ref, *outs):
+    part_ref, score_ref, grad = outs
     grad[...] = jnp.dot(scaled_ref[...], weight_ref[...], preferred_element_type=F32)
-    for d in range(X):
-        at = pl.multiple_of(lax.rem(own_ref[0] + d, X) * SLOTS, SLOTS)
-        parts[d][...] = grad[pl.ds(at, SLOTS), :].astype(BF16)
+    part_ref[...] = grad[...].astype(BF16)
     narrow = jnp.zeros((ROWS, LANES), F32)
     for f in range(0, FFW, LANES):
         narrow = narrow + grad[:, f : f + LANES] * acts_ref[:, f : f + LANES].astype(F32)
     score_ref[...] = jnp.sum(narrow.T, axis=0, keepdims=True)
 
 
-def act_part(own, scaled, weight, acts):
+def act_part(scaled, weight, acts):
     vmem = pl.BlockSpec(memory_space=pltpu.VMEM)
     return pl.pallas_call(
         act_kernel,
-        in_specs=[pl.BlockSpec(memory_space=pltpu.SMEM), vmem, vmem, vmem],
-        out_shape=[jax.ShapeDtypeStruct((SLOTS, FFW), BF16)] * X + [jax.ShapeDtypeStruct((1, ROWS), F32)],
+        in_specs=[vmem, vmem, vmem],
+        out_shape=[jax.ShapeDtypeStruct((ROWS, FFW), BF16)] + [jax.ShapeDtypeStruct((1, ROWS), F32)],
         scratch_shapes=[pltpu.VMEM((ROWS, FFW), F32)],
         compiler_params=pltpu.CompilerParams(vmem_limit_bytes=VMEM),
         cost_estimate=pl.CostEstimate(flops=2 * ROWS * FFW * WIDE, bytes_accessed=6 << 20, transcendentals=0),
         name="act_part",
-    )(own, scaled, weight, acts)
+    )(scaled, weight, acts)
 
 
 def shift(block, axis, n, d):
@@ -156,9 +154,10 @@
 
     *sums, scaled = weight_part(own_zb.reshape(1), recv.reshape(FAN // SUB, SUB * BLOCK, LANES), acts)
     near = [sums[0]] + [shift(sums[d], "zb", ZB, d) for d in range(1, ZB)]
-    *parts, score = act_part(own_x.reshape(1), scaled, weight, acts)
-    near[1], parts, score = lax.optimization_barrier((near[1], parts, score))
-
+    *parts, score = act_part(scaled, weight, acts)
+    raw, = parts
+    raw_parts = lax.all_to_all(raw.reshape(X, SLOTS, FFW), "x", split_axis=0, concat_axis=0, tiled=True)
+    near[1], raw_parts, score = lax.optimization_barrier((near[1], raw_parts, score))
     near = sum(part.astype(F32) for part in near)
     near = near.reshape(ZA, LANES, FFW)
     away = lax.dynamic_index_in_dim(near, 1 - own_za, 0, keepdims=False).astype(BF16)
@@ -168,9 +167,7 @@
     returned = lax.all_to_all(
         score.reshape(FAN, 1, CAP), ("x",) + EXPERT, split_axis=0, concat_axis=0, tiled=True
     )
-    hidden_grad = parts[0].astype(F32)
-    for d in range(1, X):
-        hidden_grad = hidden_grad + shift(parts[d], "x", X, d).astype(F32)
+    hidden_grad = jnp.sum(raw_parts.astype(F32), axis=0)
     gate_part = hidden_grad * up_act * sigmoid_val * (1.0 + gate_act * (1.0 - sigmoid_val))
     up_part = hidden_grad * silu_val
     gu_grad = jnp.concatenate([gate_part, up_part], axis=1).astype(BF16)

time: 281 us -> 281 us (level)
  the two profiles are of different devices: /device:TPU:64 before, /device:TPU:65 now
where the time goes in v5:
time: 281 us; the launch traced here: 280 us
  starting transfers between devices  120 us (43%)
  waiting for transfers between devices  120 us (43%)
  local copies, waits for them, and re-layouts  23.1 us (8%)
  Pallas kernels  10.3 us (4%)
  other arithmetic  6.05 us (2%)
    all_to_all x1, waiting for transfers between devices, per_device(): lax.all_to_all(rows.reshape(FAN, BLOCK, LANES), ('x',) + EXPERT, split_ax...  89.9 us
    ppermute x7, starting transfers between devices, shift(): return lax.ppermute(block, axis, [(i, (i + d) % n) for i in range(n)])  54.1 us
    all_to_all x1, starting transfers between devices, per_device(): lax.all_to_all(rows.reshape(FAN, BLOCK, LANES), ('x',) + EXPERT, split_ax...  33.6 us
    all_to_all x1, starting transfers between devices, per_device(): lax.all_to_all(score.reshape(FAN, 1, CAP), ('x',) + EXPERT, split_axis=0,...  28.1 us
    all_to_all x1, waiting for transfers between devices, per_device(): lax.all_to_all(score.reshape(FAN, 1, CAP), ('x',) + EXPERT, split_axis=0,...  16.1 us
    unnamed x39, local copies, waits for them, and re-layouts  16.1 us
    ppermute x7, waiting for transfers between devices, shift(): return lax.ppermute(block, axis, [(i, (i + d) % n) for i in range(n)])  13.6 us
  transfers between devices with their start and end apart: 10, of which 5 were waited for; matrix products, arithmetic and copies ran while one was open for 8% of the time, Pallas kernels for 0%

profile of v5, /device:TPU:65, one launch (start us, length us, event | category | flops | bytes accessed | tf_op | source)
XLA Modules:
  0.0 280.0 jit_solution(10575674590389649658)
XLA Ops:
  0.6 1.2 copy-done.2
  1.9 0.7 copy-done.9
  2.5 0.7 copy-done.11
  3.2 3.6 %pack.1 = bf16[4,1536,128]{2,1,0:T(8,128)(2,1)} custom-call(s32[1,128]{1,0:T(1,128)S(1)} %bitcast.35, bf16[1,128]{1,0:T(2,128)(2,1)S(1)} %bitcast.37, bf16[128,4096]{1,0:T(8,128)(2,1)S(1)} %copy-done.2), custom_call_target="tpu_custom_call" | custom-call | flops 1610612736 | bytes 3145728 | tf_op jit(solution)/shard_map/pack/pallas_call | solution.py:52
  6.8 33.6 %all-to-all-start = ((bf16[128,48,128]{2,1,0:T(8,128)(2,1)}), bf16[128,48,128]{2,1,0:T(8,128)(2,1)S(1)}, u32[]{:S(2)}, u32[]{:S(2)}) async-start(bf16[128,48,128]{2,1,0:T(8,128)(2,1)} %bitcast.3), calls=%async_computation | async-start | bytes 3145728 | tf_op jit(solution)/shard_map/all_to_all | solution.py:133
  40.4 1.5 constant_dynamic-slice_fusion.1
  42.1 0.5 copy-done.10
  42.6 0.2 fusion
  42.8 0.3 copy-done.13
  43.0 0.2 fusion.1
  43.2 5.0 %collective-permute-start = (bf16[192,768]{1,0:T(8,128)(2,1)S(1)}, bf16[192,768]{1,0:T(8,128)(2,1)}, u32[]{:S(2)}, u32[]{:S(2)}) collective-permute-start(bf16[192,768]{1,0:T(8,128)(2,1)S(1)} %fusion.1), channel_id=1, source_target_pairs={{0,96},{32,0},{64,32},{96,64},{1,97},{33,1},{65,33},{97,65},{2,98}... | collective-permute-start | bytes 884744 | tf_op jit(solution)/shard_map/ppermute | solution.py:127
  48.3 2.0 collective-permute-start.1
  50.3 2.7 collective-permute-start.2
  53.0 0.7 constant_dynamic-update-slice_fusion.7
  53.8 7.5 %collective-permute-done = bf16[192,768]{1,0:T(8,128)(2,1)} collective-permute-done((bf16[192,768]{1,0:T(8,128)(2,1)S(1)}, bf16[192,768]{1,0:T(8,128)(2,1)}, u32[]{:S(2)}, u32[]{:S(2)}) %collective-permute-start) | collective-permute-done | bytes 294944 | tf_op jit(solution)/shard_map/ppermute | solution.py:127
  61.2 1.7 constant_dynamic-update-slice_fusion.6
  62.9 1.7 constant_dynamic-update-slice_fusion.5
  64.6 3.3 %collective-permute-done.2 = bf16[192,768]{1,0:T(8,128)(2,1)} collective-permute-done((bf16[192,768]{1,0:T(8,128)(2,1)S(1)}, bf16[192,768]{1,0:T(8,128)(2,1)}, u32[]{:S(2)}, u32[]{:S(2)}) %collective-permute-start.2) | collective-permute-done | bytes 294944 | tf_op jit(solution)/shard_map/ppermute | solution.py:127
  67.9 1.7 constant_dynamic-update-slice_fusion.4
  69.6 0.7 constant_dynamic-update-slice_fusion.3
  70.3 1.7 constant_dynamic-update-slice_fusion.2
  72.0 1.7 constant_dynamic-update-slice_fusion.1
  73.7 1.7 constant_dynamic-update-slice_fusion
  75.4 2.4 constant_dynamic-slice_fusion.acts_ref
  77.8 89.9 %all-to-all-done = bf16[128,48,128]{2,1,0:T(8,128)(2,1)S(1)} async-done(((bf16[128,48,128]{2,1,0:T(8,128)(2,1)}), bf16[128,48,128]{2,1,0:T(8,128)(2,1)S(1)}, u32[]{:S(2)}, u32[]{:S(2)}) %all-to-all-start) | async-done | bytes 1572896 | tf_op jit(solution)/shard_map/all_to_all | solution.py:133
  167.7 1.3 copy-done
  169.0 4.3 %weight_part.1 = (bf16[256,768]{1,0:T(8,128)(2,1)S(1)}, bf16[256,768]{1,0:T(8,128)(2,1)S(1)}, bf16[256,768]{1,0:T(8,128)(2,1)S(1)}, bf16[256,768]{1,0:T(8,128)(2,1)S(1)}, bf16[768,1024]{1,0:T(8,128)(2,1)S(1)}) custom-call(s32[1]{0:T(128)} %bitcast.own_ref, bf16[8,768,128]{2,1,0:T(8,128)(2,1)S(1)} %bitcast.33, bf16[768,768]{1,0:T(8,128)(2,1)S(1)} %copy-done), custom_call_target="tpu_custom_call" | custom-call | flops 2415919104 | bytes 6291456 | tf_op jit(solution)/shard_map/weight_part/pallas_call | solution.py:92
  173.3 0.7 copy-done.3
  174.1 0.7 copy-done.7
  174.8 2.4 act_part.1
  177.3 3.9 %all-to-all-start.1 = ((bf16[4,192,768]{2,1,0:T(8,128)(2,1)}), bf16[4,192,768]{2,1,0:T(8,128)(2,1)S(1)}, u32[]{:S(2)}, u32[]{:S(2)}) async-start(bf16[4,192,768]{2,1,0:T(8,128)(2,1)} %bitcast.11), calls=%async_computation.1 | async-start | bytes 2359296 | tf_op jit(solution)/shard_map/all_to_all | solution.py:159
  181.2 31.8 %collective-permute-start.3 = (bf16[256,768]{1,0:T(8,128)(2,1)S(1)}, bf16[256,768]{1,0:T(8,128)(2,1)S(1)}, u32[]{:S(2)}, u32[]{:S(2)}) collective-permute-start(bf16[256,768]{1,0:T(8,128)(2,1)S(1)} %copy-done.8), channel_id=1, source_target_pairs={{0,128},{128,256},{256,384},{384,0},{1,129},{129,257},{257,385},{3... | collective-permute-start | bytes 1179656 | tf_op jit(solution)/shard_map/ppermute | solution.py:127
  213.0 4.0 %collective-permute-start.4 = (bf16[256,768]{1,0:T(8,128)(2,1)S(1)}, bf16[256,768]{1,0:T(8,128)(2,1)}, u32[]{:S(2)}, u32[]{:S(2)}) collective-permute-start(bf16[256,768]{1,0:T(8,128)(2,1)S(1)} %copy-done.6), channel_id=1, source_target_pairs={{0,256},{128,384},{256,0},{384,128},{1,257},{129,385},{257,1},{385... | collective-permute-start | bytes 1179656 | tf_op jit(solution)/shard_map/ppermute | solution.py:127
  217.0 1.9 collective-permute-start.5
  218.9 2.8 %collective-permute-done.3 = bf16[256,768]{1,0:T(8,128)(2,1)S(1)} collective-permute-done((bf16[256,768]{1,0:T(8,128)(2,1)S(1)}, bf16[256,768]{1,0:T(8,128)(2,1)S(1)}, u32[]{:S(2)}, u32[]{:S(2)}) %collective-permute-start.3) | collective-permute-done | bytes 393248 | tf_op jit(solution)/shard_map/ppermute | solution.py:127
  221.8 0.8 reshape.89
  222.6 28.1 %all-to-all-start.2 = ((f32[128,1,6]{2,1,0:T(1,128)}), f32[128,1,6]{2,1,0:T(1,128)S(1)}, u32[]{:S(2)}, u32[]{:S(2)}) async-start(f32[128,1,6]{2,1,0:T(1,128)} %bitcast.18), calls=%async_computation.2 | async-start | bytes 131072 | tf_op jit(solution)/shard_map/all_to_all | solution.py:167
  250.7 0.2 convert_reduce_fusion
  250.9 1.4 fusion.11
  252.3 1.3 convert_add_fusion
  253.6 6.6 %collective-permute-start.6 = (bf16[128,768]{1,0:T(8,128)(2,1)S(1)}, bf16[128,768]{1,0:T(8,128)(2,1)S(1)}, u32[]{:S(2)}, u32[]{:S(2)}) collective-permute-start(bf16[128,768]{1,0:T(8,128)(2,1)S(1)} %fusion.12), channel_id=1, source_target_pairs={{0,512},{512,0},{1,513},{513,1},{2,514},{514,2},{3,515},{515,3},{4... | collective-permute-start | bytes 589832 | tf_op jit(solution)/shard_map/ppermute | solution.py:127
  260.3 0.9 pad_maximum_fusion
  261.1 16.1 %all-to-all-done.2 = f32[128,1,6]{2,1,0:T(1,128)S(1)} async-done(((f32[128,1,6]{2,1,0:T(1,128)}), f32[128,1,6]{2,1,0:T(1,128)S(1)}, u32[]{:S(2)}, u32[]{:S(2)}) %all-to-all-start.2) | async-done | bytes 3104 | tf_op jit(solution)/shard_map/all_to_all | solution.py:167
  277.2 0.5 broadcast.24
  277.8 0.8 reduce.4
  278.7 0.1 select_reduce_fusion
  278.8 0.5 bitcast_divide_fusion
  279.3 0.7 fusion.13
  (35 shorter events, 0.3 us)
Async XLA Ops:
  0.6 1.2 copy-start.2
  1.9 0.7 copy-start.9
  2.5 0.7 copy-start.11
  6.8 160.9 %all-to-all-start = ((bf16[128,48,128]{2,1,0:T(8,128)(2,1)}), bf16[128,48,128]{2,1,0:T(8,128)(2,1)S(1)}, u32[]{:S(2)}, u32[]{:S(2)}) async-start(bf16[128,48,128]{2,1,0:T(8,128)(2,1)} %bitcast.3), calls=%async_computation | async-start | bytes 3145728 | tf_op jit(solution)/shard_map/all_to_all | solution.py:133
  41.9 0.7 copy-start.10
  42.0 1.1 copy-start.13
  43.2 18.0 %collective-permute-start = (bf16[192,768]{1,0:T(8,128)(2,1)S(1)}, bf16[192,768]{1,0:T(8,128)(2,1)}, u32[]{:S(2)}, u32[]{:S(2)}) collective-permute-start(bf16[192,768]{1,0:T(8,128)(2,1)S(1)} %fusion.1), channel_id=1, source_target_pairs={{0,96},{32,0},{64,32},{96,64},{1,97},{33,1},{65,33},{97,65},{2,98}... | collective-permute-start | bytes 884744 | tf_op jit(solution)/shard_map/ppermute | solution.py:127
  48.3 14.7 %collective-permute-start.1 = (bf16[192,768]{1,0:T(8,128)(2,1)S(1)}, bf16[192,768]{1,0:T(8,128)(2,1)}, u32[]{:S(2)}, u32[]{:S(2)}) collective-permute-start(bf16[192,768]{1,0:T(8,128)(2,1)S(1)} %fusion.1), channel_id=1, source_target_pairs={{0,64},{32,96},{64,0},{96,32},{1,65},{33,97},{65,1},{97,33},{2,66}... | collective-permute-start | bytes 884744 | tf_op jit(solution)/shard_map/ppermute | solution.py:127
  50.3 17.6 %collective-permute-start.2 = (bf16[192,768]{1,0:T(8,128)(2,1)S(1)}, bf16[192,768]{1,0:T(8,128)(2,1)}, u32[]{:S(2)}, u32[]{:S(2)}) collective-permute-start(bf16[192,768]{1,0:T(8,128)(2,1)S(1)} %fusion.1), channel_id=1, source_target_pairs={{0,32},{32,64},{64,96},{96,0},{1,33},{33,65},{65,97},{97,1},{2,34}... | collective-permute-start | bytes 884744 | tf_op jit(solution)/shard_map/ppermute | solution.py:127
  167.7 1.3 copy-start
  169.0 5.8 %copy-start.1 = (bf16[768,768]{1,0:T(8,128)(2,1)S(1)}, bf16[768,768]{1,0:T(8,128)(2,1)}, u32[]{:S(2)}) copy-start(bf16[768,768]{1,0:T(8,128)(2,1)} %constant_dynamic-slice_fusion.acts_ref) | copy-start | bytes 3538948
  173.3 0.7 copy-start.3
  174.1 0.7 copy-start.7
  174.8 2.4 copy-start.5
  174.8 6.4 %copy-start.8 = (bf16[256,768]{1,0:T(8,128)(2,1)S(1)}, bf16[256,768]{1,0:T(8,128)(2,1)}, u32[]{:S(2)}) copy-start(bf16[256,768]{1,0:T(8,128)(2,1)} %copy-done.7) | copy-start | bytes 1179652
  174.8 42.2 %copy-start.4 = (bf16[256,768]{1,0:T(8,128)(2,1)S(1)}, bf16[256,768]{1,0:T(8,128)(2,1)}, u32[]{:S(2)}) copy-start(bf16[256,768]{1,0:T(8,128)(2,1)} %copy-done.3) | copy-start | bytes 1179652
  177.2 35.7 %copy-start.6 = (bf16[256,768]{1,0:T(8,128)(2,1)S(1)}, bf16[256,768]{1,0:T(8,128)(2,1)}, u32[]{:S(2)}) copy-start(bf16[256,768]{1,0:T(8,128)(2,1)} %copy-done.5) | copy-start | bytes 1179652
  177.3 44.5 %all-to-all-start.1 = ((bf16[4,192,768]{2,1,0:T(8,128)(2,1)}), bf16[4,192,768]{2,1,0:T(8,128)(2,1)S(1)}, u32[]{:S(2)}, u32[]{:S(2)}) async-start(bf16[4,192,768]{2,1,0:T(8,128)(2,1)} %bitcast.11), calls=%async_computation.1 | async-start | bytes 2359296 | tf_op jit(solution)/shard_map/all_to_all | solution.py:159
  181.2 40.6 %collective-permute-start.3 = (bf16[256,768]{1,0:T(8,128)(2,1)S(1)}, bf16[256,768]{1,0:T(8,128)(2,1)S(1)}, u32[]{:S(2)}, u32[]{:S(2)}) collective-permute-start(bf16[256,768]{1,0:T(8,128)(2,1)S(1)} %copy-done.8), channel_id=1, source_target_pairs={{0,128},{128,256},{256,384},{384,0},{1,129},{129,257},{257,385},{3... | collective-permute-start | bytes 1179656 | tf_op jit(solution)/shard_map/ppermute | solution.py:127
  213.0 39.3 %collective-permute-start.4 = (bf16[256,768]{1,0:T(8,128)(2,1)S(1)}, bf16[256,768]{1,0:T(8,128)(2,1)}, u32[]{:S(2)}, u32[]{:S(2)}) collective-permute-start(bf16[256,768]{1,0:T(8,128)(2,1)S(1)} %copy-done.6), channel_id=1, source_target_pairs={{0,256},{128,384},{256,0},{384,128},{1,257},{129,385},{257,1},{385... | collective-permute-start | bytes 1179656 | tf_op jit(solution)/shard_map/ppermute | solution.py:127
  217.0 35.3 %collective-permute-start.5 = (bf16[256,768]{1,0:T(8,128)(2,1)S(1)}, bf16[256,768]{1,0:T(8,128)(2,1)}, u32[]{:S(2)}, u32[]{:S(2)}) collective-permute-start(bf16[256,768]{1,0:T(8,128)(2,1)S(1)} %copy-done.4), channel_id=1, source_target_pairs={{0,384},{128,0},{256,128},{384,256},{1,385},{129,1},{257,129},{385... | collective-permute-start | bytes 1179656 | tf_op jit(solution)/shard_map/ppermute | solution.py:127
  221.8 0.8 copy-start.14
  222.6 54.7 %all-to-all-start.2 = ((f32[128,1,6]{2,1,0:T(1,128)}), f32[128,1,6]{2,1,0:T(1,128)S(1)}, u32[]{:S(2)}, u32[]{:S(2)}) async-start(f32[128,1,6]{2,1,0:T(1,128)} %bitcast.18), calls=%async_computation.2 | async-start | bytes 131072 | tf_op jit(solution)/shard_map/all_to_all | solution.py:167
  250.7 1.6 copy-start.15
  252.3 26.5 %copy-start.12 = (bf16[128,1]{0,1:T(2,128)(2,1)S(1)}, bf16[128,1]{0,1:T(2,128)(2,1)}, u32[]{:S(2)}) copy-start(bf16[128,1]{0,1:T(2,128)(2,1)} %param.7) | copy-start | bytes 772
  253.6 25.7 %collective-permute-start.6 = (bf16[128,768]{1,0:T(8,128)(2,1)S(1)}, bf16[128,768]{1,0:T(8,128)(2,1)S(1)}, u32[]{:S(2)}, u32[]{:S(2)}) collective-permute-start(bf16[128,768]{1,0:T(8,128)(2,1)S(1)} %fusion.12), channel_id=1, source_target_pairs={{0,512},{512,0},{1,513},{513,1},{2,514},{514,2},{3,515},{515,3},{4... | collective-permute-start | bytes 589832 | tf_op jit(solution)/shard_map/ppermute | solution.py:127
